TPU v7x, 128 devices: a whole 4x4x4 slice. The times are simulated.
128 devices in a mesh: slab: 8 (over y, core), cross: 16 (over x, z).
Axes of the slice: x: 4, y: 4, z: 4, core: 2. Of those that a mesh axis runs over, the one named last changes fastest.
Arguments:
- state: float32 [22, 512, 4096], P(None, ('slab', 'cross')), may hold values from -6 to 6
- velocity: float32 [3, 512, 4096], P(None, ('slab', 'cross')), may hold values from -3 to 3
- history: float32 [22, 512, 4096], P(None, ('slab', 'cross')), may hold values from -6 to 6
- diffusion: float32 [22], replicated, may hold values from 0.05 to 0.5
- box_target: int32 [8, 64], P('slab', 'cross'), may hold values from 0 to 63, as said below
- parcel_mass: float32 [524288], P(('slab', 'cross')), may hold values from 0.2 to 2
- parcel_state: float32 [5, 524288], P(None, ('slab', 'cross')), may hold values from -6 to 6
- parcel_box: int32 [524288], P(('slab', 'cross')), may hold values from 0 to 511, as said below
- parcel_cell: int32 [524288], P(('slab', 'cross')), may hold values from 0 to 4095
- parcel_count: int32 [128], P(('slab', 'cross')), may hold values from 1024 to 4096, as said below
Outputs:
- new_state: float32 [22, 512, 4096], P(None, ('slab', 'cross'))
- tendency: float32 [22, 512, 4096], P(None, ('slab', 'cross'))
Inputs may be any that keep to these rules, and one draw needn't show every extreme that they name: `box_target`: within each slab group every new owner and slot receives exactly one box, and the 4 boxes of one device go to 4 different owners. The owner device is parcel_box // 4. On each device the parcels of one owner stand together. At most 64 parcels of one device go to one owner, and some owner receives 64 live parcels from every device. `parcel_count`: A multiple of 128; parcels below the count are live, the others are padding; some device is full.
All inputs are finite; a program needn't handle non-finite values.
Results may differ from a plain program's by a relative error of at most 0.000082.
Values sent between devices are 32-bit elements; how exact they have to be, the bound alone decides.
A program may use at most 192 MiB of HBM per device.

v0:
```python
import jax
import jax.numpy as jnp
from jax import lax
from jax.sharding import PartitionSpec as P

BE = 16
PAR_DEV = 4096


TIME_STEP = 0.2
LATENT = 0.5
DEPOSIT = 0.25


def padded(block, sides, width, periodic):
    for axis, dim in sides:
        count = lax.axis_size(axis)
        forward = [(i, i + 1) for i in range(count - 1)]
        if periodic:
            forward.append((count - 1, 0))
        backward = [(target, source) for source, target in forward]
        low = lax.ppermute(
            lax.slice_in_dim(block, block.shape[dim] - width, None, axis=dim), axis, forward
        )
        high = lax.ppermute(lax.slice_in_dim(block, 0, width, axis=dim), axis, backward)
        block = jnp.concatenate([low, block, high], axis=dim)
    return block


def to_brick(boxes, box_count):
    count = boxes.shape[0]
    shaped = boxes.reshape(count, box_count, BE, BE, BE)
    return shaped.transpose(0, 2, 3, 1, 4).reshape(count, BE, BE, box_count * BE)


def from_brick(brick, box_count):
    count = brick.shape[0]
    shaped = brick.reshape(count, BE, BE, box_count, BE)
    return shaped.transpose(0, 3, 1, 2, 4).reshape(count, box_count, BE * BE * BE)


def face_flux(coeff, low_q, high_q, low_g, high_g, low_u, high_u):
    return coeff * (0.5 * (low_g + high_g)) * (high_q - low_q) - 0.5 * (low_u + high_u) * (
        0.5 * (low_q + high_q)
    )


def per_device(
    state,
    velocity,
    history,
    diffusion,
    box_target,
    parcel_mass,
    parcel_state,
    parcel_box,
    parcel_cell,
    parcel_count,
):
    fields = state.shape[0]
    box_count = state.shape[1]
    cells_here = box_count * BE * BE * BE
    cross_size = lax.axis_size("cross")
    slab_size = lax.axis_size("slab")
    total_devices = slab_size * cross_size
    capacity = 2 * PAR_DEV // total_devices
    width = total_devices * capacity
    live = jnp.arange(PAR_DEV, dtype=jnp.int32) < parcel_count[0]
    destination = jnp.where(live, parcel_box // box_count, total_devices)
    order = jnp.argsort(destination, stable=True)
    ranked = destination[order]
    first_seen = jnp.searchsorted(ranked, ranked, side="left")
    rank_within = jnp.arange(PAR_DEV, dtype=jnp.int32) - first_seen
    slot_sorted = jnp.where(ranked < total_devices, ranked * capacity + rank_within, width)
    send_slot = jnp.zeros((PAR_DEV,), jnp.int32).at[order].set(slot_sorted)
    local_cell = parcel_box % box_count * (BE * BE * BE) + parcel_cell
    mass_out = jnp.zeros((1, width), jnp.float32).at[0, send_slot].set(parcel_mass, mode="drop")
    state_out = jnp.zeros((5, width), jnp.float32).at[:, send_slot].set(parcel_state, mode="drop")
    cell_out = jnp.full((1, width), -1, jnp.int32).at[0, send_slot].set(local_cell, mode="drop")
    mass_in, state_in, cell_in = (
        lax.all_to_all(mass_out, ("slab", "cross"), split_axis=1, concat_axis=1, tiled=True),
        lax.all_to_all(state_out, ("slab", "cross"), split_axis=1, concat_axis=1, tiled=True),
        lax.all_to_all(cell_out, ("slab", "cross"), split_axis=1, concat_axis=1, tiled=True),
    )
    targets = box_target[0]
    owners = targets // box_count
    new_slots = targets % box_count
    peers = jnp.arange(cross_size, dtype=jnp.int32)
    match = owners[None, :] == peers[:, None]
    picked = jnp.sum(jnp.where(match, jnp.arange(box_count, dtype=jnp.int32)[None, :], 0), axis=1)
    present = jnp.any(match, axis=1)
    slot_send = jnp.where(present, jnp.sum(jnp.where(match, new_slots[None, :], 0), axis=1), -1)[
        None, :
    ]

    def outgoing(array):
        return jnp.where(present[None, :, None], jnp.take(array, picked, axis=1), jnp.float32(0.0))

    def place(arrived, incoming_slots):
        hit = incoming_slots[0][None, :] == jnp.arange(box_count, dtype=jnp.int32)[:, None]
        source = jnp.sum(jnp.where(hit, peers[None, :], 0), axis=1)
        return jnp.take(arrived, source, axis=1)

    got_state, got_velocity, got_history, got_slots = (
        lax.all_to_all(outgoing(state), "cross", split_axis=1, concat_axis=1, tiled=True),
        lax.all_to_all(outgoing(velocity), "cross", split_axis=1, concat_axis=1, tiled=True),
        lax.all_to_all(outgoing(history), "cross", split_axis=1, concat_axis=1, tiled=True),
        lax.all_to_all(slot_send, "cross", split_axis=1, concat_axis=1, tiled=True),
    )
    placed_history = place(got_history, got_slots)
    placed_state = place(got_state, got_slots)
    placed_velocity = place(got_velocity, got_slots)
    combined = to_brick(jnp.concatenate([placed_state, placed_velocity], axis=0), box_count)
    along_z = padded(combined, (("slab", 2),), 1, True)
    along_x = padded(combined, (("cross", 1),), 1, False)
    coeff = diffusion[:, None, None, None]

    def spread_of(block):
        return 1.0 + 0.5 * jnp.tanh(block[fields - 1])

    values = along_x[:fields]
    grow = spread_of(along_x)
    stream = along_x[fields]
    flux_x = face_flux(
        coeff, values[:, :-1], values[:, 1:], grow[:-1], grow[1:], stream[:-1], stream[1:]
    )
    face_index = jnp.arange(BE + 1)
    cross_here = lax.axis_index("cross")
    wall = (face_index == 0) & (cross_here == 0) | (face_index == BE) & (
        cross_here == cross_size - 1
    )
    flux_x = jnp.where(wall[None, :, None, None], jnp.float32(0.0), flux_x)
    total = flux_x[:, 1:] - flux_x[:, :-1]
    values = along_z[:fields]
    grow = spread_of(along_z)
    stream = along_z[fields + 2]
    flux_z = face_flux(
        coeff,
        values[:, :, :-1],
        values[:, :, 1:],
        grow[:, :-1],
        grow[:, 1:],
        stream[:, :-1],
        stream[:, 1:],
    )
    total = total + flux_z[:, :, 1:] - flux_z[:, :, :-1]
    values = combined[:fields]
    grow = spread_of(combined)
    stream = combined[fields + 1]
    flux_y = face_flux(
        coeff,
        values[..., :-1],
        values[..., 1:],
        grow[..., :-1],
        grow[..., 1:],
        stream[..., :-1],
        stream[..., 1:],
    )
    padded_y = jnp.pad(flux_y, ((0, 0), (0, 0), (0, 0), (1, 1)))
    total = total + padded_y[..., 1:] - padded_y[..., :-1]
    tendency = from_brick(total, box_count)
    advanced = placed_state + TIME_STEP * (1.5 * tendency - 0.5 * placed_history)
    valid = cell_in[0] >= 0
    where_at = jnp.maximum(cell_in[0], 0)
    flat_state = advanced.reshape(fields, cells_here)
    flat_velocity = placed_velocity.reshape(3, cells_here)
    fuel = jnp.take(flat_state[0], where_at)
    energy = jnp.take(flat_state[fields - 1], where_at)
    gas_flow = jnp.take(flat_velocity, where_at, axis=1)
    slip = jnp.sum((gas_flow - state_in[2:5]) ** 2, axis=0)
    coef = jnp.where(valid, mass_in[0] * jnp.sqrt(1.0 + slip), jnp.float32(0.0))
    rate = coef * (state_in[0] - fuel)
    heat = coef * (state_in[1] - energy) - LATENT * rate
    fuel_source = jnp.zeros((cells_here,), jnp.float32).at[where_at].add(rate)
    heat_source = jnp.zeros((cells_here,), jnp.float32).at[where_at].add(heat)
    new_state = advanced.at[0].add(DEPOSIT * fuel_source.reshape(box_count, -1))
    new_state = new_state.at[fields - 1].add(DEPOSIT * heat_source.reshape(box_count, -1))
    return (new_state, tendency)


def solution(mesh):
    return jax.shard_map(
        per_device,
        mesh=mesh,
        in_specs=(
            P(None, ("slab", "cross"), None),
            P(None, ("slab", "cross"), None),
            P(None, ("slab", "cross"), None),
            P(),
            P("slab", "cross"),
            P(("slab", "cross")),
            P(None, ("slab", "cross")),
            P(("slab", "cross")),
            P(("slab", "cross")),
            P(("slab", "cross")),
        ),
        out_specs=(P(None, ("slab", "cross"), None), P(None, ("slab", "cross"), None)),
        check_vma=False,
    )
```

profile of v0, /device:TPU:1, one launch (start us, length us, event | category | flops | bytes accessed | tf_op | source)
XLA Modules:
  0.0 1045.5 jit_solution(8615603415675161318)
XLA Ops:
  2.3 8.4 all-to-all-start.1
  12.2 5.8 sort.17
  18.0 23.0 %gather_fusion.3 = s32[4096]{0:T(1024)S(1)} fusion(s32[4096]{0:T(1024)S(1)} %get-tuple-element.157, s32[4096]{0:T(1024)S(1)} %get-tuple-element.158), kind=kCustom, calls=%fused_computation.9 | custom fusion | bytes 49152 | tf_op jit(solution)/shard_map/gather | solution.py:71
  41.0 300.6 %while.27 = (s32[]{:T(128)}, u32[4096]{0:T(1024)S(1)}, u32[4096]{0:T(1024)S(1)}, s32[4096]{0:T(1024)S(1)}, s32[]{:T(128)}, /*index=5*/s32[]{:T(128)}, s32[]{}) while((s32[]{:T(128)}, u32[4096]{0:T(1024)S(1)}, u32[4096]{0:T(1024)S(1)}, s32[4096]{0:T(1024)S(1)}, s32[]{:T(128)}, /*index=5*/s32[]{:T(128)}, s32[]{}) %tuple.73), condition=%wide.region_6.9_spmd.clone, body=%wide.region_5.8_spmd.clone.sunk | while | flops 77828 | bytes 270437 | solution.py:72
  41.1 23.0 %gather_fusion = s32[4096]{0:T(1024)S(1)} fusion(s32[4096]{0:T(1024)S(1)} %get-tuple-element.214, u32[4096]{0:T(1024)S(1)} %broadcast_clamp_fusion.4), kind=kCustom, calls=%fused_computation.2.clone.clone.1 | custom fusion | bytes 49152 | tf_op jit(solution)/shard_map/jit(searchsorted)/jit(_searchsorted_scan_impl)/vmap(jit(_searchsorted_scan_impl))/while/body/eval_jaxpr/gather | solution.py:72
  64.2 23.0 %gather_fusion = s32[4096]{0:T(1024)S(1)} fusion(s32[4096]{0:T(1024)S(1)} %get-tuple-element.214, u32[4096]{0:T(1024)S(1)} %broadcast_clamp_fusion.4), kind=kCustom, calls=%fused_computation.2.clone.clone.1 | custom fusion | bytes 49152 | tf_op jit(solution)/shard_map/jit(searchsorted)/jit(_searchsorted_scan_impl)/vmap(jit(_searchsorted_scan_impl))/while/body/eval_jaxpr/gather | solution.py:72
  87.3 23.0 %gather_fusion = s32[4096]{0:T(1024)S(1)} fusion(s32[4096]{0:T(1024)S(1)} %get-tuple-element.214, u32[4096]{0:T(1024)S(1)} %broadcast_clamp_fusion.4), kind=kCustom, calls=%fused_computation.2.clone.clone.1 | custom fusion | bytes 49152 | tf_op jit(solution)/shard_map/jit(searchsorted)/jit(_searchsorted_scan_impl)/vmap(jit(_searchsorted_scan_impl))/while/body/eval_jaxpr/gather | solution.py:72
  110.5 23.0 %gather_fusion = s32[4096]{0:T(1024)S(1)} fusion(s32[4096]{0:T(1024)S(1)} %get-tuple-element.214, u32[4096]{0:T(1024)S(1)} %broadcast_clamp_fusion.4), kind=kCustom, calls=%fused_computation.2.clone.clone.1 | custom fusion | bytes 49152 | tf_op jit(solution)/shard_map/jit(searchsorted)/jit(_searchsorted_scan_impl)/vmap(jit(_searchsorted_scan_impl))/while/body/eval_jaxpr/gather | solution.py:72
  133.6 23.0 %gather_fusion = s32[4096]{0:T(1024)S(1)} fusion(s32[4096]{0:T(1024)S(1)} %get-tuple-element.214, u32[4096]{0:T(1024)S(1)} %broadcast_clamp_fusion.4), kind=kCustom, calls=%fused_computation.2.clone.clone.1 | custom fusion | bytes 49152 | tf_op jit(solution)/shard_map/jit(searchsorted)/jit(_searchsorted_scan_impl)/vmap(jit(_searchsorted_scan_impl))/while/body/eval_jaxpr/gather | solution.py:72
  156.7 23.0 %gather_fusion = s32[4096]{0:T(1024)S(1)} fusion(s32[4096]{0:T(1024)S(1)} %get-tuple-element.214, u32[4096]{0:T(1024)S(1)} %broadcast_clamp_fusion.4), kind=kCustom, calls=%fused_computation.2.clone.clone.1 | custom fusion | bytes 49152 | tf_op jit(solution)/shard_map/jit(searchsorted)/jit(_searchsorted_scan_impl)/vmap(jit(_searchsorted_scan_impl))/while/body/eval_jaxpr/gather | solution.py:72
  179.8 23.0 %gather_fusion = s32[4096]{0:T(1024)S(1)} fusion(s32[4096]{0:T(1024)S(1)} %get-tuple-element.214, u32[4096]{0:T(1024)S(1)} %broadcast_clamp_fusion.4), kind=kCustom, calls=%fused_computation.2.clone.clone.1 | custom fusion | bytes 49152 | tf_op jit(solution)/shard_map/jit(searchsorted)/jit(_searchsorted_scan_impl)/vmap(jit(_searchsorted_scan_impl))/while/body/eval_jaxpr/gather | solution.py:72
  203.0 23.0 %gather_fusion = s32[4096]{0:T(1024)S(1)} fusion(s32[4096]{0:T(1024)S(1)} %get-tuple-element.214, u32[4096]{0:T(1024)S(1)} %broadcast_clamp_fusion.4), kind=kCustom, calls=%fused_computation.2.clone.clone.1 | custom fusion | bytes 49152 | tf_op jit(solution)/shard_map/jit(searchsorted)/jit(_searchsorted_scan_impl)/vmap(jit(_searchsorted_scan_impl))/while/body/eval_jaxpr/gather | solution.py:72
  226.1 23.0 %gather_fusion = s32[4096]{0:T(1024)S(1)} fusion(s32[4096]{0:T(1024)S(1)} %get-tuple-element.214, u32[4096]{0:T(1024)S(1)} %broadcast_clamp_fusion.4), kind=kCustom, calls=%fused_computation.2.clone.clone.1 | custom fusion | bytes 49152 | tf_op jit(solution)/shard_map/jit(searchsorted)/jit(_searchsorted_scan_impl)/vmap(jit(_searchsorted_scan_impl))/while/body/eval_jaxpr/gather | solution.py:72
  249.2 23.0 %gather_fusion = s32[4096]{0:T(1024)S(1)} fusion(s32[4096]{0:T(1024)S(1)} %get-tuple-element.214, u32[4096]{0:T(1024)S(1)} %broadcast_clamp_fusion.4), kind=kCustom, calls=%fused_computation.2.clone.clone.1 | custom fusion | bytes 49152 | tf_op jit(solution)/shard_map/jit(searchsorted)/jit(_searchsorted_scan_impl)/vmap(jit(_searchsorted_scan_impl))/while/body/eval_jaxpr/gather | solution.py:72
  272.3 23.0 %gather_fusion = s32[4096]{0:T(1024)S(1)} fusion(s32[4096]{0:T(1024)S(1)} %get-tuple-element.214, u32[4096]{0:T(1024)S(1)} %broadcast_clamp_fusion.4), kind=kCustom, calls=%fused_computation.2.clone.clone.1 | custom fusion | bytes 49152 | tf_op jit(solution)/shard_map/jit(searchsorted)/jit(_searchsorted_scan_impl)/vmap(jit(_searchsorted_scan_impl))/while/body/eval_jaxpr/gather | solution.py:72
  295.5 23.0 %gather_fusion = s32[4096]{0:T(1024)S(1)} fusion(s32[4096]{0:T(1024)S(1)} %get-tuple-element.214, u32[4096]{0:T(1024)S(1)} %broadcast_clamp_fusion.4), kind=kCustom, calls=%fused_computation.2.clone.clone.1 | custom fusion | bytes 49152 | tf_op jit(solution)/shard_map/jit(searchsorted)/jit(_searchsorted_scan_impl)/vmap(jit(_searchsorted_scan_impl))/while/body/eval_jaxpr/gather | solution.py:72
  318.6 23.0 %gather_fusion = s32[4096]{0:T(1024)S(1)} fusion(s32[4096]{0:T(1024)S(1)} %get-tuple-element.214, u32[4096]{0:T(1024)S(1)} %broadcast_clamp_fusion.4), kind=kCustom, calls=%fused_computation.2.clone.clone.1 | custom fusion | bytes 49152 | tf_op jit(solution)/shard_map/jit(searchsorted)/jit(_searchsorted_scan_impl)/vmap(jit(_searchsorted_scan_impl))/while/body/eval_jaxpr/gather | solution.py:72
  341.7 15.5 %scatter_custom_fusion = s32[4096]{0:T(1024)S(1)} fusion(s32[4096]{0:T(1024)S(1)} %get-tuple-element.159, s32[4096]{0:T(1024)S(1)} %add_select_fusion.2, s32[]{:T(128)} %constant.238.clone.1), kind=kCustom, calls=%fused_computation.131 | custom fusion | bytes 16388 | tf_op jit(solution)/shard_map/scatter | solution.py:75
  357.5 15.7 %scatter_custom_fusion.5 = f32[8192]{0:T(1024)S(1)} fusion(s32[4096]{0:T(1024)S(1)} %broadcast_select_fusion.1, f32[4096]{0:T(1024)} %param.27, f32[]{:T(128)} %constant.243.clone.1), kind=kCustom, calls=%fused_computation.118 | custom fusion | bytes 33280
  374.0 10.3 all-to-all-start.5
  384.3 15.5 %scatter_custom_fusion.4 = s32[8192]{0:T(1024)S(1)} fusion(s32[4096]{0:T(1024)S(1)} %broadcast_select_fusion.1, s32[4096]{0:T(1024)S(1)} %get-tuple-element.156, s32[]{:T(128)} %constant.241.clone.1), kind=kCustom, calls=%fused_computation.120 | custom fusion | bytes 32772
  402.3 9.8 all-to-all-start.4
  414.2 13.1 %scatter_custom_fusion.1 = f32[5,8192]{0,1:T(8,128)} fusion(s32[4096]{0:T(1024)S(1)} %compare_select_fusion.1, f32[4096,5]{1,0:T(8,128)} %copy.201, f32[]{:T(128)} %constant.243.clone.1), kind=kCustom, calls=%fused_computation.44 | custom fusion | bytes 164352 | tf_op jit(solution)/shard_map/scatter | solution.py:78
  427.2 3.0 copy.202
  431.2 10.0 all-to-all-start.6
  442.7 11.0 %gather_fusion.7 = f32[16,22,4096]{2,0,1:T(8,128)} fusion(f32[22,4,4096]{2,1,0:T(4,128)S(1)} %copy-done, s32[1024]{0:T(1024)S(1)} %pad_clamp_fusion.3), kind=kCustom, calls=%fused_computation.4.clone | custom fusion | bytes 11534400 | tf_op jit(solution)/shard_map/jit(_take)/gather | solution.py:97
  453.7 11.4 %gather_fusion.5 = f32[16,22,4096]{2,0,1:T(8,128)} fusion(f32[22,4,4096]{2,1,0:T(4,128)S(1)} %copy-done.2, s32[1024]{0:T(1024)S(1)} %pad_clamp_fusion.3), kind=kCustom, calls=%fused_computation.clone | custom fusion | bytes 11534400 | tf_op jit(solution)/shard_map/jit(_take)/gather | solution.py:97
  465.0 7.1 all-to-all-start.2
  472.1 8.7 bitcast_select_fusion
  480.8 5.9 copy.171
  487.8 5.8 all-to-all-start
  493.6 8.7 copy.191
  510.9 5.1 copy.199
  516.0 71.7 %all-to-all-done = f32[22,16,4096]{2,0,1:T(8,128)} async-done(((f32[22,16,4096]{2,0,1:T(8,128)}), f32[22,16,4096]{2,0,1:T(8,128)}, u32[]{:S(2)}, u32[]{:S(2)}) %all-to-all-start) | async-done | bytes 5767200 | tf_op jit(solution)/shard_map/all_to_all | solution.py:105
  587.7 8.6 all-to-all-start.3
  596.3 13.1 %broadcast_select_fusion = f32[3,16384]{0,1:T(8,128)} fusion(f32[3,16384]{0,1:T(8,128)} %copy.199, pred[16384]{0:T(1024)(128)(4,1)S(1)} %bitcast.103), kind=kLoop, calls=%fused_computation.42 | loop fusion | flops 49152 | bytes 409600 | tf_op jit(solution)/shard_map/jit(_take)/select_n | solution.py:102
  609.4 31.1 %gather_fusion.4 = f32[8192,3]{1,0:T(8,128)} fusion(f32[3,16384]{0,1:T(8,128)} %broadcast_select_fusion, s32[8192]{0:T(1024)S(1)} %get-tuple-element.154), kind=kCustom, calls=%fused_computation.10 | custom fusion | bytes 229376 | tf_op jit(solution)/shard_map/jit(_take)/gather | solution.py:169
  640.4 3.0 copy.200
  644.6 3.4 gather_fusion.6
  648.5 2.2 copy.173
  650.7 8.6 reshape.265
  659.3 15.1 %copy.174 = f32[25,16,16,4,16]{0,4,3,2,1:T(8,128)} copy(f32[25,16,16,4,16]{4,2,1,3,0:T(8,128)} %bitcast.86) | data formatting | bytes 3276800 | tf_op jit(solution)/shard_map/transpose | solution.py:33
  674.4 9.9 slice.272
  686.8 13.9 %copy.204 = f32[22,16,16,4,16]{0,4,3,2,1:T(8,128)} copy(f32[22,16,16,4,16]{4,2,1,3,0:T(8,128)} %slice.272) | data formatting | bytes 2883584 | tf_op jit(solution)/shard_map/slice | solution.py:147
  700.7 2.3 fusion.54
  703.0 4.8 collective-permute-start.2
  707.8 2.3 fusion.53
  710.2 3.7 collective-permute-start
  715.3 11.5 %multiply_subtract_fusion.1 = f32[22,16,16,63]{0,3,2,1:T(8,128)} fusion(f32[22,16,16,64]{0,3,2,1:T(8,128)} %bitcast.89, f32[16,16,63]{2,1,0:T(8,128)S(1)} %get-tuple-element.164, f32[16,16,63]{2,1,0:T(8,128)S(1)} %get-tuple-element.165, f32[22]{0:T(128)} %param.25), kind=kLoop, calls=%fused_computation.39 | loop fusion | flops 2128896 | bytes 4386904 | tf_op jit(solution)/shard_map/sub | solution.py:43
  726.8 7.1 copy.176
  733.8 7.1 copy.179
  740.9 4.6 gather_fusion.8
  752.4 11.9 %fusion.2 = f32[17,16,64]{2,1,0:T(8,128)S(1)} fusion(f32[25,1,16,64]{0,3,2,1:T(8,128)S(1)} %collective-permute-done.1, f32[25,16,16,64]{0,3,2,1:T(8,128)} %bitcast.81, f32[25,1,16,64]{0,3,2,1:T(8,128)S(1)} %collective-permute-done), kind=kLoop, calls=%fused_computation.28 | loop fusion | flops 69632 | bytes 1912832 | tf_op jit(solution)/shard_map/mul | solution.py:43
  764.4 11.8 %multiply_subtract_fusion = f32[22,16,17,64]{0,3,2,1:T(8,128)} fusion(f32[25,16,1,64]{0,3,2,1:T(8,128)} %collective-permute-done.3, f32[25,16,16,64]{0,3,2,1:T(8,128)} %bitcast.82, f32[25,16,1,64]{0,3,2,1:T(8,128)S(1)} %collective-permute-done.2, f32[16,17,64]{2,1,0:T(8,128)S(1)} %copy.182, f32[16,17,64]{2,1,0:T(8,128)S(1)} %copy.181, f32[22]{0:T(128)S(1)} %copy-done.16), kind=kLoop, calls=%fused_computation.32 | loop fusion | flops 3063808 | bytes 3514456 | tf_op jit(solution)/shard_map/sub | solution.py:43
  776.2 7.1 subtract_select_fusion
  783.4 21.8 %fusion.4 = f32[22,16,16,64]{0,3,2,1:T(8,128)} fusion(f32[22,16,16,63]{0,3,2,1:T(8,128)} %multiply_subtract_fusion.1, f32[22,16,17,64]{0,3,2,1:T(8,128)} %multiply_subtract_fusion, f32[22,17,16,64]{0,3,2,1:T(8,128)} %subtract_select_fusion), kind=kLoop, calls=%fused_computation.35 | loop fusion | flops 1802240 | bytes 8628224 | tf_op jit(solution)/shard_map/sub | solution.py:160
  805.1 16.6 %copy.206 = f32[22,16,16,4,16]{4,3,2,1,0:T(4,128)} copy(f32[22,16,16,4,16]{0,4,3,2,1:T(8,128)} %bitcast.91) | data formatting | bytes 2883584 | tf_op jit(solution)/shard_map/reshape | solution.py:38
  821.7 10.2 copy.189
  831.9 8.7 reshape.268
  841.7 2.5 fusion.9
  845.5 45.5 %gather_fusion.9 = f32[8192]{0:T(1024)S(1)} fusion(f32[16384]{0:T(1024)S(1)} %bitcast.76, s32[8192]{0:T(1024)S(1)} %copy-done.10), kind=kCustom, calls=%fused_computation.3.clone | custom fusion | bytes 98304 | tf_op jit(solution)/shard_map/jit(_take)/gather | solution.py:167
  891.1 45.5 %gather_fusion.10 = f32[8192]{0:T(1024)S(1)} fusion(f32[16384]{0:T(1024)S(1)} %bitcast.75, s32[8192]{0:T(1024)S(1)} %copy-done.10), kind=kCustom, calls=%fused_computation.6.clone | custom fusion | bytes 98304 | tf_op jit(solution)/shard_map/jit(_take)/gather | solution.py:168
  936.8 52.6 %scatter_custom_fusion.3 = f32[16384]{0:T(1024)S(1)} fusion(s32[8192]{0:T(1024)S(1)} %copy-done.9, f32[8192]{0:T(1024)S(1)} %get-tuple-element.140, f32[]{:T(128)} %constant.243.clone.1), kind=kCustom, calls=%fused_computation.101 | custom fusion | flops 8192 | bytes 65540 | tf_op jit(solution)/shard_map/scatter-add | solution.py:175
  989.4 52.6 %scatter_custom_fusion.2 = f32[16384]{0:T(1024)S(1)} fusion(s32[8192]{0:T(1024)S(1)} %copy-done.9, f32[8192]{0:T(1024)S(1)} %get-tuple-element.141, f32[]{:T(128)} %constant.243.clone.1), kind=kCustom, calls=%fused_computation.103 | custom fusion | flops 8192 | bytes 65540 | tf_op jit(solution)/shard_map/scatter-add | solution.py:174
  (196 shorter events, 38.1 us)
Async XLA Ops:
  0.6 442.0 %copy-start = (f32[22,4,4096]{2,1,0:T(4,128)S(1)}, f32[22,4,4096]{2,1,0:T(4,128)}, u32[]{:S(2)}) copy-start(f32[22,4,4096]{2,1,0:T(4,128)} %param.24) | copy-start | bytes 4325380
  2.3 371.7 %all-to-all-start.1 = ((s32[1,16,1]{2,0,1:T(1,128)}), s32[1,16,1]{2,0,1:T(1,128)S(1)}, u32[]{:S(2)}, u32[]{:S(2)}) async-start(s32[1,16,1]{2,0,1:T(1,128)} %copy.170), calls=%async_computation.1 | async-start | bytes 16384 | tf_op jit(solution)/shard_map/all_to_all | solution.py:108
  41.0 316.3 %copy-start.19 = (s32[2]{0:T(128)S(1)}, s32[2]{0:T(128)}, u32[]{:S(2)}) copy-start(s32[2]{0:T(128)} %constant.274) | copy-start | bytes 28
  41.0 316.4 %copy-start.18 = (s32[2]{0:T(128)S(1)}, s32[2]{0:T(128)}, u32[]{:S(2)}) copy-start(s32[2]{0:T(128)} %constant.271) | copy-start | bytes 28
  41.0 359.5 %copy-start.3 = (f32[3,4,4096]{2,1,0:T(4,128)S(1)}, f32[3,4,4096]{2,1,0:T(4,128)}, u32[]{:S(2)}) copy-start(f32[3,4,4096]{2,1,0:T(4,128)} %param.23) | copy-start | bytes 589828
  341.7 70.5 %copy-start.11 = (f32[5,4096]{1,0:T(8,128)S(1)}, f32[5,4096]{1,0:T(8,128)}, u32[]{:S(2)}) copy-start(f32[5,4096]{1,0:T(8,128)} %param.28) | copy-start | bytes 245764
  374.0 28.3 %all-to-all-start.5 = ((f32[1,128,64]{2,0,1:T(1,128)}), f32[1,128,64]{2,0,1:T(1,128)S(1)}, u32[]{:S(2)}, u32[]{:S(2)}) async-start(f32[1,128,64]{2,0,1:T(1,128)} %bitcast.24), calls=%async_computation.5 | async-start | bytes 131072 | tf_op jit(solution)/shard_map/all_to_all | solution.py:81
  402.3 28.9 %all-to-all-start.4 = ((s32[1,128,64]{2,0,1:T(1,128)}), s32[1,128,64]{2,0,1:T(1,128)S(1)}, u32[]{:S(2)}, u32[]{:S(2)}) async-start(s32[1,128,64]{2,0,1:T(1,128)} %bitcast.23), calls=%async_computation.4 | async-start | bytes 131072 | tf_op jit(solution)/shard_map/all_to_all | solution.py:83
  431.2 33.9 %all-to-all-start.6 = ((f32[128,1,320]{2,1,0:T(1,128)}), f32[128,1,320]{2,1,0:T(1,128)S(1)}, u32[]{:S(2)}, u32[]{:S(2)}) async-start(f32[128,1,320]{2,1,0:T(1,128)} %reshape.474), calls=%async_computation.6 | async-start | bytes 393216 | tf_op jit(solution)/shard_map/all_to_all | solution.py:82
  442.7 11.0 %copy-start.2 = (f32[22,4,4096]{2,1,0:T(4,128)S(1)}, f32[22,4,4096]{2,1,0:T(4,128)}, u32[]{:S(2)}) copy-start(f32[22,4,4096]{2,1,0:T(4,128)} %param.22) | copy-start | bytes 4325380
  465.0 22.8 %all-to-all-start.2 = ((f32[3,16,4096]{2,0,1:T(4,128)}), f32[3,16,4096]{2,0,1:T(4,128)S(1)}, u32[]{:S(2)}, u32[]{:S(2)}) async-start(f32[3,16,4096]{2,0,1:T(4,128)} %copy.172), calls=%async_computation.2 | async-start | bytes 2097152 | tf_op jit(solution)/shard_map/all_to_all | solution.py:106
  487.8 99.9 %all-to-all-start = ((f32[22,16,4096]{2,0,1:T(8,128)}), f32[22,16,4096]{2,0,1:T(8,128)}, u32[]{:S(2)}, u32[]{:S(2)}) async-start(f32[22,16,4096]{2,0,1:T(8,128)} %copy.171), calls=%async_computation | async-start | bytes 12582912 | tf_op jit(solution)/shard_map/all_to_all | solution.py:105
  506.1 81.5 %copy-start.8 = (s32[8192]{0:T(1024)}, s32[8192]{0:T(1024)S(1)}, u32[]{:S(2)}) copy-start(s32[8192]{0:T(1024)S(1)} %reshape.387) | copy-start | bytes 98308
  587.7 153.2 %all-to-all-start.3 = ((f32[22,16,4096]{2,0,1:T(8,128)}), f32[22,16,4096]{2,0,1:T(8,128)}, u32[]{:S(2)}, u32[]{:S(2)}) async-start(f32[22,16,4096]{2,0,1:T(8,128)} %copy.191), calls=%async_computation.3 | async-start | bytes 12582912 | tf_op jit(solution)/shard_map/all_to_all | solution.py:107
  703.0 45.4 %collective-permute-start.2 = (f32[25,16,1,64]{0,3,2,1:T(8,128)}, f32[25,16,1,64]{0,3,2,1:T(8,128)S(1)}, u32[]{:S(2)}, u32[]{:S(2)}) collective-permute-start(f32[25,16,1,64]{0,3,2,1:T(8,128)} %get-tuple-element.146), channel_id=1, source_target_pairs={{0,16},{16,32},{32,48},{48,64},{64,80},{80,96},{96,112},{112,0},{1... | collective-permute-start | bytes 307208 | tf_op jit(solution)/shard_map/ppermute | solution.py:22
  707.8 41.4 %collective-permute-start.3 = (f32[25,16,1,64]{0,3,2,1:T(8,128)}, f32[25,16,1,64]{0,3,2,1:T(8,128)}, u32[]{:S(2)}, u32[]{:S(2)}) collective-permute-start(f32[25,16,1,64]{0,3,2,1:T(8,128)} %get-tuple-element.147), channel_id=1, source_target_pairs={{16,0},{32,16},{48,32},{64,48},{80,64},{96,80},{112,96},{0,112},{1... | collective-permute-start | bytes 307208 | tf_op jit(solution)/shard_map/ppermute | solution.py:25
  710.2 35.4 %collective-permute-start = (f32[25,1,16,64]{0,3,2,1:T(8,128)}, f32[25,1,16,64]{0,3,2,1:T(8,128)S(1)}, u32[]{:S(2)}, u32[]{:S(2)}) collective-permute-start(f32[25,1,16,64]{0,3,2,1:T(8,128)} %get-tuple-element.144), channel_id=1, source_target_pairs={{0,1},{1,2},{2,3},{3,4},{4,5},{5,6},{6,7},{7,8},{8,9},{9,10},{10,1... | collective-permute-start | bytes 307208 | tf_op jit(solution)/shard_map/ppermute | solution.py:22
  713.8 32.0 %collective-permute-start.1 = (f32[25,1,16,64]{0,3,2,1:T(8,128)}, f32[25,1,16,64]{0,3,2,1:T(8,128)S(1)}, u32[]{:S(2)}, u32[]{:S(2)}) collective-permute-start(f32[25,1,16,64]{0,3,2,1:T(8,128)} %get-tuple-element.145), channel_id=1, source_target_pairs={{1,0},{2,1},{3,2},{4,3},{5,4},{6,5},{7,6},{8,7},{9,8},{10,9},{11,1... | collective-permute-start | bytes 307208 | tf_op jit(solution)/shard_map/ppermute | solution.py:25
  747.7 16.6 %copy-start.16 = (f32[22]{0:T(128)S(1)}, f32[22]{0:T(128)}, u32[]{:S(2)}) copy-start(f32[22]{0:T(128)} %param.25) | copy-start | bytes 268
  752.4 23.8 %slice-start = ((s8[8388608]{0:T(1024)(128)(4,1)}), s8[4194304]{0:T(1024)(128)(4,1)S(1)}, s32[]{:S(2)}) async-start(s8[8388608]{0:T(1024)(128)(4,1)} %bitcast.83), calls=%async_computation.7 | async-start | bytes 8388608
  764.3 11.9 %slice-start.1 = ((s8[8388608]{0:T(1024)(128)(4,1)}), s8[4194304]{0:T(1024)(128)(4,1)S(1)}, s32[]{:S(2)}) async-start(s8[8388608]{0:T(1024)(128)(4,1)} %bitcast.83), calls=%async_computation.8 | async-start | bytes 8388608
  764.3 11.9 %copy-start.7 = (f32[17,16,64]{2,1,0:T(8,128)S(1)}, f32[17,16,64]{2,1,0:T(8,128)}, u32[]{:S(2)}) copy-start(f32[17,16,64]{2,1,0:T(8,128)} %fusion.24) | copy-start | bytes 208900
  764.3 11.9 %copy-start.17 = (pred[17]{0:T(512)(128)(4,1)S(1)}, pred[17]{0:T(512)(128)(4,1)}, u32[]{:S(2)}) copy-start(pred[17]{0:T(512)(128)(4,1)} %and_or_fusion) | copy-start | bytes 55
  831.9 13.6 %copy-start.10 = (s32[8192]{0:T(1024)S(1)}, s32[8192]{0:T(1024)}, u32[]{:S(2)}) copy-start(s32[8192]{0:T(1024)} %get-tuple-element.155) | copy-start | bytes 98308
  840.6 1.1 copy-start.6
  844.3 1.2 copy-start.4
  891.1 45.6 %copy-start.9 = (s32[8192]{0:T(1024)S(1)}, s32[8192]{0:T(1024)}, u32[]{:S(2)}) copy-start(s32[8192]{0:T(1024)} %copy-done.8) | copy-start | bytes 98308
  891.1 45.6 %copy-start.12 = (f32[8192]{0:T(1024)S(1)}, f32[8192]{0:T(1024)}, u32[]{:S(2)}) copy-start(f32[8192]{0:T(1024)} %squeeze.41) | copy-start | bytes 98308
  891.1 45.6 %copy-start.13 = (f32[8192]{0:T(1024)S(1)}, f32[8192]{0:T(1024)}, u32[]{:S(2)}) copy-start(f32[8192]{0:T(1024)} %squeeze.44) | copy-start | bytes 98308
  891.1 45.6 %copy-start.14 = (f32[8192]{0:T(1024)S(1)}, f32[8192]{0:T(1024)}, u32[]{:S(2)}) copy-start(f32[8192]{0:T(1024)} %squeeze.42) | copy-start | bytes 98308
  891.1 45.6 %copy-start.15 = (f32[8192]{0:T(1024)S(1)}, f32[8192]{0:T(1024)}, u32[]{:S(2)}) copy-start(f32[8192]{0:T(1024)} %sqrt.7) | copy-start | bytes 98308
  891.1 150.9 %copy-start.5 = (f32[22,4,4096]{2,0,1:T(8,128)S(1)}, f32[22,4,4096]{2,0,1:T(8,128)}, u32[]{:S(2)}) copy-start(f32[22,4,4096]{2,0,1:T(8,128)} %copy-done.4) | copy-start | bytes 4325380
  891.1 153.9 %copy-start.1 = (f32[22,4,4096]{2,1,0:T(4,128)S(1)}, f32[22,4,4096]{2,1,0:T(4,128)}, u32[]{:S(2)}) copy-start(f32[22,4,4096]{2,1,0:T(4,128)} %param.24) | copy-start | bytes 4325380
where the time goes:
time: 1060 us; the launch traced here: 1050 us
  local copies, waits for them, and re-layouts  689 us (65%)
  other arithmetic  211 us (20%)
  waiting for transfers between devices  72.7 us (7%)
  starting transfers between devices  69.8 us (7%)
    gather x13, local copies, waits for them, and re-layouts, per_device(): first_seen = jnp.searchsorted(ranked, ranked, side='left')  299 us
    all_to_all x1, waiting for transfers between devices, per_device(): lax.all_to_all(outgoing(state), 'cross', split_axis=1, concat_axis=1, til...  71.7 us
    scatter-add x1, other arithmetic, per_device(): heat_source = jnp.zeros((cells_here,), jnp.float32).at[where_at].add(heat)  52.6 us
    scatter-add x1, other arithmetic, per_device(): fuel_source = jnp.zeros((cells_here,), jnp.float32).at[where_at].add(rate)  52.6 us
    gather x1, local copies, waits for them, and re-layouts, per_device(): fuel = jnp.take(flat_state[0], where_at)  45.5 us
    gather x1, local copies, waits for them, and re-layouts, per_device(): energy = jnp.take(flat_state[fields - 1], where_at)  45.5 us
    unnamed x52, local copies, waits for them, and re-layouts  38.8 us
    gather x2, local copies, waits for them, and re-layouts, per_device(): gas_flow = jnp.take(flat_velocity, where_at, axis=1)  34.1 us
  transfers between devices with their start and end apart: 11, of which 2 were waited for; matrix products, arithmetic and copies ran while one was open for 57% of the time, Pallas kernels for 0%

commit v1 on v0

v1 whole, which is shorter than its diff:
```python
import functools

import jax
import jax.numpy as jnp
from jax import lax
from jax.experimental import pallas as pl
from jax.experimental.pallas import tpu as pltpu
from jax.sharding import PartitionSpec as P

MESH = pl.DeviceIdType.MESH
F32 = jnp.float32
BF16 = jnp.bfloat16

BE = 16
PAR_DEV = 4096
CAP = 64
FIELDS = 22
N_SLAB = 8
N_CROSS = 16
CHUNK = 512

TIME_STEP = 0.2
LATENT = 0.5
DEPOSIT = 0.25

GROUPS = (
    ((1, 0, 3), (0, 0, 10)),
    ((0, 10, 12),),
    ((2, 0, 11),),
    ((2, 11, 11),),
)
WIDTHS = (13, 12, 11, 11)


def iota(dim, shape=(8, 128)):
    return lax.broadcasted_iota(jnp.int32, shape, dim)


def lane_roll(x, shift):
    shift = shift % 128
    return x if shift == 0 else pltpu.roll(x, shift, x.ndim - 1)


def sub_roll(x, shift):
    shift = shift % 8
    return x if shift == 0 else pltpu.roll(x, shift, x.ndim - 2)


def pack_kernel(start_ref, len_ref, w_ref, out_ref):
    lane = iota(1)
    row = iota(0)

    def body(o, carry):
        start = start_ref[o]
        base = pl.multiple_of((start // 128) * 128, 128)
        window = w_ref[:, pl.ds(base, 256)]
        window = pltpu.roll(window, 256 - (start - base), 1)[:, :128]
        window = jnp.where((row == 0) & (lane >= len_ref[o]), 0.0, window)
        low = window[0:4]
        high = pltpu.roll(window, 64, 1)[4:8]
        out_ref[o % N_CROSS, o // N_CROSS] = jnp.where(lane[0:4] < 64, low, high)
        return carry

    lax.fori_loop(0, N_SLAB * N_CROSS, body, 0, unroll=4)


def pack(start, length, w):
    return pl.pallas_call(
        pack_kernel,
        out_shape=jax.ShapeDtypeStruct((N_CROSS, N_SLAB, 4, 128), F32),
        in_specs=[
            pl.BlockSpec(memory_space=pltpu.SMEM),
            pl.BlockSpec(memory_space=pltpu.SMEM),
            pl.BlockSpec(memory_space=pltpu.VMEM),
        ],
        out_specs=pl.BlockSpec(memory_space=pltpu.VMEM),
    )(start, length, w)


def mix_kernel(*refs):
    (s_ref, v_ref, h_ref, tg_ref, sb_ref) = refs[:5]
    arrays = (s_ref, v_ref, h_ref)
    placed = refs[5:9]
    (xl, xh, zl, zh, z0, z15, r2) = refs[9:16]
    bufs = refs[16:20]
    outs = refs[20:24]
    (tgb, inv_v, inv_s, r1) = refs[24:28]
    (tsem, p1, p2, hsem, psem, lsem) = refs[28:34]

    me_s = lax.axis_index("slab")
    me_c = lax.axis_index("cross")

    def cross(d):
        return lax.rem(me_c + d, N_CROSS)

    def slab(d):
        return lax.rem(me_s + d, N_SLAB)

    barrier = pltpu.get_barrier_semaphore()

    def greet_c(d, carry):
        pl.semaphore_signal(barrier, inc=1, device_id=(me_s, cross(d)), device_id_type=MESH)
        return carry

    def greet_s(d, carry):
        pl.semaphore_signal(barrier, inc=1, device_id=(slab(d), me_c), device_id_type=MESH)
        return carry

    lax.fori_loop(1, N_CROSS, greet_c, 0)
    lax.fori_loop(1, N_SLAB, greet_s, 0)
    pl.semaphore_wait(barrier, N_CROSS - 1 + N_SLAB - 1)

    def remote(src, dst, sems, peer):
        return pltpu.make_async_remote_copy(
            src_ref=src,
            dst_ref=dst,
            send_sem=sems.at[0],
            recv_sem=sems.at[1],
            device_id=peer,
            device_id_type=MESH,
        )

    def drain(ref, sem):
        pltpu.make_async_copy(ref, ref, sem).wait()

    def send_targets(d, carry):
        remote(tg_ref, tgb.at[me_c], tsem, (me_s, cross(d))).start()
        return carry

    lax.fori_loop(1, N_CROSS, send_targets, 0)
    tgb[me_c] = tg_ref[...]

    def parts(g):
        at = 0
        for which, first, count in GROUPS[g]:
            yield arrays[which], first, count, at
            at += count

    def phase1(g):
        sems = p1.at[g]

        def body(d, carry):
            m = cross(d)
            for src, first, count, at in parts(g):
                remote(
                    src.at[pl.ds(first, count), m],
                    bufs[g].at[me_c, pl.ds(at, count)],
                    sems,
                    (me_s, m),
                ).start()
            return carry

        lax.fori_loop(1, N_CROSS, body, 0)
        for src, first, count, at in parts(g):
            pltpu.make_async_copy(
                src.at[pl.ds(first, count), me_c], bufs[g].at[me_c, pl.ds(at, count)], lsem.at[g]
            ).start()

    def phase2(g):
        width = WIDTHS[g]
        sems = p1.at[g]
        drain(bufs[g].at[pl.ds(0, N_CROSS - 1)], sems.at[1])
        drain(bufs[g].at[0], lsem.at[g])

        def fill(t):
            for q in range(4):
                code = inv_s[t * 4 + q, 0] & 63
                outs[g][t, :, q : q + 5 : 4, :] = bufs[g][
                    lax.div(code, 4), :, pl.ds(lax.rem(code, 4), 2, stride=4), :
                ]

        def body(d, carry):
            t = cross(d)
            fill(t)
            remote(outs[g].at[t], placed[g].at[me_c], p2.at[g], (me_s, t)).start()
            return carry

        lax.fori_loop(1, N_CROSS, body, 0)
        fill(me_c)
        pltpu.make_async_copy(outs[g].at[me_c], placed[g].at[me_c], lsem.at[g]).start()

    def landed(g):
        drain(placed[g].at[pl.ds(0, N_CROSS - 1)], p2.at[g, 1])
        drain(placed[g].at[0], lsem.at[g])

    def sent(g):
        drain(bufs[g].at[pl.ds(0, N_CROSS - 1)], p1.at[g, 0])
        drain(outs[g].at[pl.ds(0, N_CROSS - 1)], p2.at[g, 0])

    phase1(0)
    phase1(1)

    drain(tgb.at[pl.ds(0, N_CROSS - 1)], tsem.at[1])
    flat = tgb[0]
    for s in range(1, N_CROSS):
        flat = flat + tgb[s]
    for tile in range(8):
        hit = flat == iota(0) + 8 * tile
        code = jnp.sum(jnp.where(hit & (iota(1) < 64), iota(1).astype(F32), 0.0), axis=1, keepdims=True)
        inv_v[8 * tile : 8 * tile + 8, :] = jnp.broadcast_to(code, (8, 128)).astype(jnp.int32)
    to_scalar = pltpu.make_async_copy(inv_v, inv_s, lsem.at[4])
    to_scalar.start()
    to_scalar.wait()

    phase2(0)

    def parcels1(d, carry):
        c = cross(d)
        remote(sb_ref.at[c], r1.at[me_c], psem.at[0], (me_s, c)).start()
        return carry

    lax.fori_loop(1, N_CROSS, parcels1, 0)
    own = pltpu.make_async_copy(sb_ref.at[me_c], r1.at[me_c], lsem.at[4])
    own.start()
    phase1(2)
    phase2(1)
    phase1(3)

    own.wait()
    drain(r1.at[pl.ds(0, N_CROSS - 1)], psem.at[0, 1])

    def parcels2(d, carry):
        a = slab(d)
        remote(r1.at[:, a], r2.at[me_s], psem.at[1], (a, me_c)).start()
        return carry

    lax.fori_loop(1, N_SLAB, parcels2, 0)
    own = pltpu.make_async_copy(r1.at[:, me_s], r2.at[me_s], lsem.at[4])
    own.start()

    landed(0)
    landed(1)
    x_lo = (me_s, cross(N_CROSS - 1))
    x_hi = (me_s, cross(1))
    halo = []
    for g in range(2):
        at = pl.ds(sum(WIDTHS[:g]), WIDTHS[g])
        halo.append(remote(placed[g].at[0], xh.at[at], hsem.at[g], x_lo))
        halo.append(remote(placed[g].at[BE - 1], xl.at[at], hsem.at[2 + g], x_hi))
    for copy in halo:
        copy.start()
    pack_z(placed, z0, z15)
    z_lo = (slab(N_SLAB - 1), me_c)
    z_hi = (slab(1), me_c)
    for copy in (remote(z0, zh, hsem.at[4], z_lo), remote(z15, zl, hsem.at[5], z_hi)):
        copy.start()
        halo.append(copy)

    phase2(2)
    phase2(3)
    for copy in halo:
        copy.wait()
    own.wait()
    drain(r2.at[pl.ds(0, N_SLAB - 1)], psem.at[1, 1])
    landed(2)
    landed(3)

    drain(tgb.at[pl.ds(0, N_CROSS - 1)], tsem.at[0])
    drain(r1.at[pl.ds(0, N_CROSS - 1)], psem.at[0, 0])
    drain(r2.at[pl.ds(0, N_SLAB - 1)], psem.at[1, 0])
    for g in range(4):
        sent(g)


def pack_z(placed, z0, z15):
    lane16 = iota(1) // 16
    upper = iota(0) >= 4

    for g in range(2):
        first = sum(WIDTHS[:g])

        def body(f, carry):
            low = [None, None]
            high = [None, None]
            for ih in range(2):
                for il in range(8):
                    x = placed[g][ih * 8 + il, f]
                    a = lane_roll(x, 16 * il)
                    b = lane_roll(x, 16 * il + 16)
                    if il == 0:
                        low[ih], high[ih] = a, b
                    else:
                        low[ih] = jnp.where(lane16 == il, a, low[ih])
                        high[ih] = jnp.where(lane16 == il, b, high[ih])
            z0[first + f] = jnp.where(upper, sub_roll(low[1], 4), low[0])
            z15[first + f] = jnp.where(upper, high[1], sub_roll(high[0], 4))
            return carry

        lax.fori_loop(0, WIDTHS[g], body, 0)


def mix(state, velocity, history, targets, sendbuf):
    vm = pl.BlockSpec(memory_space=pltpu.VMEM)
    hbm = pl.BlockSpec(memory_space=pl.ANY)
    total = WIDTHS[0] + WIDTHS[1]
    group = [(N_CROSS, w, 8, 128) for w in WIDTHS]
    outs = group + [(total, 8, 128)] * 6 + [(N_SLAB, N_CROSS, 4, 128)]
    return pl.pallas_call(
        mix_kernel,
        out_shape=[jax.ShapeDtypeStruct(s, F32) for s in outs],
        in_specs=[hbm, hbm, hbm, vm, vm],
        out_specs=[vm] * len(outs),
        scratch_shapes=[pltpu.VMEM(s, F32) for s in group + group]
        + [
            pltpu.VMEM((N_CROSS, 8, 128), jnp.int32),
            pltpu.VMEM((64, 128), jnp.int32),
            pltpu.SMEM((64, 128), jnp.int32),
            pltpu.VMEM((N_CROSS, N_SLAB, 4, 128), F32),
            pltpu.SemaphoreType.DMA((2,)),
            pltpu.SemaphoreType.DMA((4, 2)),
            pltpu.SemaphoreType.DMA((4, 2)),
            pltpu.SemaphoreType.DMA((6, 2)),
            pltpu.SemaphoreType.DMA((2, 2)),
            pltpu.SemaphoreType.DMA((5,)),
        ],
        compiler_params=pltpu.CompilerParams(
            collective_id=0, has_side_effects=True, vmem_limit_bytes=40 * 2**20
        ),
    )(state, velocity, history, targets, sendbuf)


def spread_of(e):
    return 1.0 + 0.5 * jnp.tanh(e)


def finish_kernel(
    d_ref, p0, p1, p2, p3, xl, xh, zl, zh, z0, z15, r2, new_ref, tend_ref,
    gx, hx, gy, hy, gz, hz, gzp, hzp, vals, tabs,
):
    me_c = lax.axis_index("cross")
    lane = iota(1)
    row = iota(0)
    kl7 = lane >= 112
    kl0 = lane < 16
    top = kl7 & (row >= 4)
    bottom = kl0 & (row < 4)
    j15 = lane % 16 == 15
    j0 = lane % 16 == 0
    wall_y = j15 & (row % 4 == 3)

    def up_z(q):
        return lane_roll(jnp.where(kl0, sub_roll(q, 4), q), -16)

    def down_z(q):
        return lane_roll(jnp.where(kl7, sub_roll(q, 4), q), 16)

    def up_y(q):
        return jnp.where(j15, sub_roll(lane_roll(q, 15), -1), lane_roll(q, -1))

    def down_y(q):
        return jnp.where(j0, sub_roll(lane_roll(q, -15), 1), lane_roll(q, 1))

    def put_top(packed, i):
        ih, il = divmod(i, 8)
        return lane_roll(packed[1 - ih], 112 - 16 * il)

    def put_bottom(packed, i):
        ih, il = divmod(i, 8)
        return lane_roll(packed[ih], -16 * il)

    E = WIDTHS[1] - 1
    EH = WIDTHS[0] + WIDTHS[1] - 1
    first_wall = jnp.where(me_c == 0, 0.0, 1.0)
    last_wall = jnp.where(me_c == N_CROSS - 1, 0.0, 1.0)
    before_g = spread_of(xl[EH])
    before_u = xl[0]
    for i in range(BE + 1):
        if i < BE:
            now_g, now_u = spread_of(p1[i, E]), p0[i, 0]
        else:
            now_g, now_u = spread_of(xh[EH]), xh[0]
        g, h = 0.5 * (before_g + now_g), 0.25 * (before_u + now_u)
        if i == 0:
            g, h = g * first_wall, h * first_wall
        if i == BE:
            g, h = g * last_wall, h * last_wall
        gx[i], hx[i] = g, h
        before_g, before_u = now_g, now_u
        if i < BE:
            uy, uz = p0[i, 1], p0[i, 2]
            gy[i] = jnp.where(wall_y, 0.0, 0.5 * (now_g + up_y(now_g)))
            hy[i] = jnp.where(wall_y, 0.0, 0.25 * (uy + up_y(uy)))
            gz[i] = 0.5 * (now_g + up_z(now_g))
            hz[i] = 0.25 * (uz + up_z(uz))
    gzp[0] = 0.5 * (spread_of(zl[EH]) + spread_of(z0[EH]))
    gzp[1] = 0.5 * (spread_of(z15[EH]) + spread_of(zh[EH]))
    hzp[0] = 0.25 * (zl[2] + z0[2])
    hzp[1] = 0.25 * (z15[2] + zh[2])

    def flux(d, g, h, low, high):
        return (d * g) * (high - low) - h * (high + low)

    def transport(q_ref, h_ref, q_at, x_at, h_at, out_at, count):
        def body(n, carry):
            f = out_at + n
            d = d_ref[f]
            xf = x_at + n
            qf = q_at + n
            edge0 = flux(d, gzp[0], hzp[0], zl[xf], z0[xf])
            edge15 = flux(d, gzp[1], hzp[1], z15[xf], zh[xf])
            edge0 = (edge0, sub_roll(edge0, 4))
            edge15 = (edge15, sub_roll(edge15, 4))
            q = q_ref[0, qf]
            fx = flux(d, gx[0], hx[0], xl[xf], q)
            for i in range(BE):
                ahead = q_ref[i + 1, qf] if i < BE - 1 else xh[xf]
                fx_up = flux(d, gx[i + 1], hx[i + 1], q, ahead)
                total = fx_up - fx
                fz = flux(d, gz[i], hz[i], q, up_z(q))
                fz = jnp.where(top, put_top(edge15, i), fz)
                fz_low = jnp.where(bottom, put_bottom(edge0, i), down_z(fz))
                total = total + fz - fz_low
                fy = flux(d, gy[i], hy[i], q, up_y(q))
                total = total + fy - down_y(fy)
                tend_ref[f, i] = total
                old = h_ref[i, h_at + n]
                new_ref[f, i] = q + TIME_STEP * (1.5 * total - 0.5 * old)
                fx = fx_up
                q = ahead
            return carry

        lax.fori_loop(0, count, body, 0)

    transport(p0, p2, 3, 3, 0, 0, 10)
    transport(p1, p2, 0, 13, 10, 10, 1)
    transport(p1, p3, 1, 14, 0, 11, 11)

    tables = [new_ref[0], new_ref[FIELDS - 1]] + [p0[:, d] for d in range(3)]
    for n, table in enumerate(tables):
        table = table.reshape(128, 128)
        first = table.astype(BF16)
        tabs[128 * n : 128 * n + 128, 0:128] = first
        tabs[128 * n : 128 * n + 128, 128:256] = (table - first.astype(F32)).astype(BF16)

    half = iota(1, (4, 128)) < 64

    def unpack(n, carry):
        a, b = r2[n // 8, 2 * (n % 8)], r2[n // 8, 2 * (n % 8) + 1]
        at = pl.ds(pl.multiple_of(n * 128, 128), 128)
        vals[0:4, at] = jnp.where(half, a, pltpu.roll(b, 64, 1))
        vals[4:8, at] = jnp.where(half, pltpu.roll(a, 64, 1), b)
        return carry

    lax.fori_loop(0, 64, unpack, 0, unroll=4)

    number = lax.broadcasted_iota(jnp.int32, (128, CHUNK), 0).astype(F32)

    def deposit(n, acc):
        v = vals[:, pl.ds(pl.multiple_of(n * CHUNK, CHUNK), CHUNK)]
        at_row = number == v[3:4]
        at_lane = jnp.where(number == v[7:8], 1.0, 0.0).astype(BF16)
        picked = jnp.dot(
            tabs[...], jnp.concatenate([at_lane, at_lane], axis=0), preferred_element_type=F32
        )

        def value(m):
            return jnp.sum(
                jnp.where(at_row, picked[128 * m : 128 * m + 128], 0.0), axis=0, keepdims=True
            )

        slip = (value(2) - v[4:5]) ** 2 + (value(3) - v[5:6]) ** 2 + (value(4) - v[6:7]) ** 2
        coef = v[0:1] * jnp.sqrt(1.0 + slip)
        rate = coef * (v[1:2] - value(0))
        heat = coef * (v[2:3] - value(1)) - LATENT * rate
        rows = []
        for x in (rate, heat):
            first = x.astype(BF16).astype(F32)
            rows.append(jnp.where(at_row, first, 0.0).astype(BF16))
            rows.append(jnp.where(at_row, x - first, 0.0).astype(BF16))
        return acc + lax.dot_general(
            jnp.concatenate(rows, axis=0),
            at_lane,
            (((1,), (1,)), ((), ())),
            preferred_element_type=F32,
        )

    acc = lax.fori_loop(
        0, N_SLAB * N_CROSS * CAP // CHUNK, deposit, jnp.zeros((512, 128), F32)
    )
    fuel = (acc[0:128] + acc[128:256]).reshape(BE, 8, 128)
    heat = (acc[256:384] + acc[384:512]).reshape(BE, 8, 128)
    new_ref[0] = new_ref[0] + DEPOSIT * fuel
    new_ref[FIELDS - 1] = new_ref[FIELDS - 1] + DEPOSIT * heat


def finish(diffusion, arrived):
    vm = pl.BlockSpec(memory_space=pltpu.VMEM)
    out = jax.ShapeDtypeStruct((FIELDS, BE, 8, 128), F32)
    return pl.pallas_call(
        finish_kernel,
        out_shape=[out, out],
        in_specs=[pl.BlockSpec(memory_space=pltpu.SMEM)] + [vm] * len(arrived),
        out_specs=[vm, vm],
        scratch_shapes=[pltpu.VMEM((BE + 1, 8, 128), F32)] * 2
        + [pltpu.VMEM((BE, 8, 128), F32)] * 4
        + [pltpu.VMEM((2, 8, 128), F32)] * 2
        + [
            pltpu.VMEM((8, N_SLAB * N_CROSS * CAP), F32),
            pltpu.VMEM((640, 256), BF16),
        ],
        compiler_params=pltpu.CompilerParams(vmem_limit_bytes=40 * 2**20),
    )(diffusion, *arrived)


def to_tiles(array):
    fields = array.shape[0]
    return (
        array.reshape(fields, 4, 32, 128).transpose(0, 2, 1, 3).reshape(fields, BE, 8, 128)
    )


def from_tiles(array):
    fields = array.shape[0]
    return array.reshape(fields, 32, 4, 128).transpose(0, 2, 1, 3).reshape(fields, 4, 4096)


def per_device(
    state,
    velocity,
    history,
    diffusion,
    box_target,
    parcel_mass,
    parcel_state,
    parcel_box,
    parcel_cell,
    parcel_count,
):
    position = jnp.arange(PAR_DEV, dtype=jnp.int32)
    owner = parcel_box // 4
    here = owner[None, :] == jnp.arange(N_SLAB * N_CROSS, dtype=jnp.int32)[:, None]
    start = jnp.min(jnp.where(here, position[None, :], PAR_DEV - 1), axis=1)
    length = jnp.sum((here & (position < parcel_count[0])[None, :]).astype(jnp.int32), axis=1)
    row = ((parcel_cell // 128) * 4 + parcel_box % 4).astype(F32)
    lane = (parcel_cell % 128).astype(F32)
    w = jnp.concatenate(
        [parcel_mass[None], parcel_state[0:2], row[None], parcel_state[2:5], lane[None]], axis=0
    )
    w = jnp.pad(w, ((0, 0), (0, 256)))
    sendbuf = pack(start, length, w)

    spot = jnp.arange(128, dtype=jnp.int32) - 4 * lax.axis_index("cross")
    targets = jnp.sum(
        jnp.where(spot[None, :] == jnp.arange(4, dtype=jnp.int32)[:, None], box_target[0][:, None], 0),
        axis=0,
    )
    targets = jnp.broadcast_to(targets[None, :], (8, 128))
    arrived = mix(to_tiles(state), to_tiles(velocity), to_tiles(history), targets, sendbuf)
    new_state, tendency = finish(diffusion, arrived)
    return from_tiles(new_state), from_tiles(tendency)


def solution(mesh):
    return jax.shard_map(
        per_device,
        mesh=mesh,
        in_specs=(
            P(None, ("slab", "cross"), None),
            P(None, ("slab", "cross"), None),
            P(None, ("slab", "cross"), None),
            P(),
            P("slab", "cross"),
            P(("slab", "cross")),
            P(None, ("slab", "cross")),
            P(("slab", "cross")),
            P(("slab", "cross")),
            P(("slab", "cross")),
        ),
        out_specs=(P(None, ("slab", "cross"), None), P(None, ("slab", "cross"), None)),
        check_vma=False,
    )
```

time: 1060 us -> 131 us (0.12)
  the two profiles are of different devices: /device:TPU:1 before, /device:TPU:104 now
where the time goes in v1:
time: 131 us
  Pallas kernels  119 us (91%)
  local copies, waits for them, and re-layouts  7.95 us (6%)
  other arithmetic  2.86 us (2%)
  between operations  1.32 us (1%)
    pallas_call x1, Pallas kernels, mix(): pl.pallas_call(mix_kernel, out_shape=[jax.ShapeDtypeStruct(s, F32) for s...  91.7 us
    pallas_call x1, Pallas kernels, finish(): pl.pallas_call(finish_kernel, out_shape=[out, out], in_specs=[pl.BlockSpe...  20.6 us
    pallas_call x1, Pallas kernels, pack(): pl.pallas_call(pack_kernel, out_shape=jax.ShapeDtypeStruct((N_CROSS, N_SL...  6.55 us
    unnamed x10, local copies, waits for them, and re-layouts  4.6 us

profile of v1, /device:TPU:104, one launch (start us, length us, event | category | flops | bytes accessed | tf_op | source)
XLA Modules:
  0.0 131.0 jit_solution(3438311674235228564)
XLA Ops:
  1.3 0.7 select_reduce_fusion.1
  2.0 0.9 slice.6
  3.0 0.8 fusion.4
  3.7 1.3 %convert_reduce_fusion = (s32[128]{0:T(128)}, s32[128]{0:T(128)}) fusion(s32[4096]{0:T(1024)S(1)} %get-tuple-element.32, pred[4096]{0:T(1024)(128)(4,1)S(1)} %iota_compare_fusion.1), kind=kLoop, calls=%fused_computation | loop fusion | flops 3145472 | bytes 21504 | tf_op jit(solution)/shard_map/reduce_sum | solution.py:533
  5.1 0.9 slice.7
  6.0 0.8 concatenate.3
  6.8 0.7 pad.4.w_ref
  7.5 6.6 %shard_map.113.refs_4_ = f32[16,8,4,128]{3,2,1,0:T(4,128)} custom-call(s32[128]{0:T(128)} %get-tuple-element.29.start_ref, s32[128]{0:T(128)} %get-tuple-element.28.len_ref, f32[8,4352]{1,0:T(8,128)} %pad.4.w_ref), custom_call_target="tpu_custom_call" | custom-call | tf_op jit(solution)/shard_map/pallas_call | solution.py:68
  14.1 0.0 copy-start
  14.1 1.4 %copy-done = f32[22,4,4096]{2,1,0:T(4,128)S(1)} copy-done((f32[22,4,4096]{2,1,0:T(4,128)S(1)}, f32[22,4,4096]{2,1,0:T(4,128)}, u32[]{:S(2)}) %copy-start) | copy-done | bytes 1441816
  15.4 0.0 copy-start.1
  15.4 1.4 %copy-done.1 = f32[22,4,4096]{2,1,0:T(4,128)S(1)} copy-done((f32[22,4,4096]{2,1,0:T(4,128)S(1)}, f32[22,4,4096]{2,1,0:T(4,128)}, u32[]{:S(2)}) %copy-start.1) | copy-done | bytes 1441816
  16.8 0.0 copy-start.2
  16.8 0.9 copy-done.2
  17.7 0.0 copy-start.3
  17.7 0.9 copy-done.3
  18.7 0.0 copy-start.4
  18.7 91.7 %shard_map.114 = (f32[16,13,8,128]{3,2,1,0:T(8,128)S(1)}, f32[16,12,8,128]{3,2,1,0:T(8,128)S(1)}, f32[16,11,8,128]{3,2,1,0:T(8,128)S(1)}, f32[16,11,8,128]{3,2,1...) custom-call(f32[22,16,8,128]{3,2,1,0:T(8,128)S(1)} %bitcast.31, ...), custom_call_target="tpu_custom_call" | custom-call | tf_op jit(solution)/shard_map/pallas_call | solution.py:298
  110.4 0.0 copy-done.4
  110.4 20.6 %shard_map.115 = (f32[22,16,8,128]{3,2,1,0:T(8,128)}, f32[22,16,8,128]{3,2,1,0:T(8,128)}) custom-call(f32[22]{0:T(128)S(1)} %copy-done.4, f32[16,13,8,128]{3,2,1,0:T(8,128)S(1)} %get-tuple-element.15.p0, f32[16,12,8,128]{3,2,1,0:T(8,128)S(1)} %get-tuple-element.16.p1, f32[16,11,8,128]{3,2,1,0:T(8,128)S(1)} %get-tuple-element.17.p2, ...), custom_call_target="tpu_custom_call" | custom-call | tf_op jit(solution)/shard_map/pallas_call | solution.py:489
  (3 shorter events, 0.0 us)
Async XLA Ops:
  14.1 1.4 %copy-start = (f32[22,4,4096]{2,1,0:T(4,128)S(1)}, f32[22,4,4096]{2,1,0:T(4,128)}, u32[]{:S(2)}) copy-start(f32[22,4,4096]{2,1,0:T(4,128)} %param.10) | copy-start | bytes 4325380
  15.4 1.4 %copy-start.1 = (f32[22,4,4096]{2,1,0:T(4,128)S(1)}, f32[22,4,4096]{2,1,0:T(4,128)}, u32[]{:S(2)}) copy-start(f32[22,4,4096]{2,1,0:T(4,128)} %param.12) | copy-start | bytes 4325380
  16.8 0.9 copy-start.2
  17.7 0.9 copy-start.3
  18.7 91.7 %copy-start.4 = (f32[22]{0:T(128)S(1)}, f32[22]{0:T(128)}, u32[]{:S(2)}) copy-start(f32[22]{0:T(128)} %d_ref.1) | copy-start | bytes 268

commit v2 on v1

--- a/solution.py
+++ b/solution.py
@@ -1,5 +1,3 @@
-import functools
-
 import jax
 import jax.numpy as jnp
 from jax import lax
@@ -18,6 +16,7 @@
 N_SLAB = 8
 N_CROSS = 16
 CHUNK = 512
+VMEM_LIMIT = 60 * 2**20
 
 TIME_STEP = 0.2
 LATENT = 0.5
@@ -25,11 +24,12 @@
 
 GROUPS = (
     ((1, 0, 3), (0, 0, 10)),
-    ((0, 10, 12),),
-    ((2, 0, 11),),
-    ((2, 11, 11),),
+    ((0, 10, 12), (2, 0, 1), (2, 21, 1)),
+    ((2, 1, 10),),
+    ((2, 11, 10),),
 )
-WIDTHS = (13, 12, 11, 11)
+WIDTHS = (13, 14, 10, 10)
+HALO = (13, 12)
 
 
 def iota(dim, shape=(8, 128)):
@@ -46,46 +46,81 @@
     return x if shift == 0 else pltpu.roll(x, shift, x.ndim - 2)
 
 
-def pack_kernel(start_ref, len_ref, w_ref, out_ref):
+def pack(mass, parcels, box, cell, count, w, spans_v, spans_s, sem, out):
+    def columns(n, carry):
+        at = pl.ds(pl.multiple_of(n * 128, 128), 128)
+        w[n, 0:1] = mass[:, at]
+        w[n, 1:3] = parcels[0:2, at]
+        w[n, 3:4] = ((cell[:, at] // 128) * 4 + box[:, at] % 4).astype(F32)
+        w[n, 4:7] = parcels[2:5, at]
+        w[n, 7:8] = (cell[:, at] % 128).astype(F32)
+        return carry
+
+    lax.fori_loop(0, PAR_DEV // 128, columns, 0, unroll=2)
+    w[PAR_DEV // 128] = jnp.zeros((8, 128), F32)
+
+    shape = (N_SLAB * N_CROSS, 128)
+    number = iota(0, shape)
+    lane = iota(1, shape)
+    live = count[0]
+
+    def scan(n, carry):
+        first, length = carry
+        owner = box[:, pl.ds(pl.multiple_of(n * 128, 128), 128)] // 4
+        here = owner == number
+        position = lane + n * 128
+        first = jnp.where(here, jnp.minimum(first, position), first)
+        length = length + jnp.where(here & (position < live), 1, 0)
+        return first, length
+
+    first, length = lax.fori_loop(
+        0,
+        PAR_DEV // 128,
+        scan,
+        (jnp.full(shape, PAR_DEV - 1, jnp.int32), jnp.zeros(shape, jnp.int32)),
+    )
+    first = jnp.min(first, axis=1, keepdims=True)
+    length = jnp.sum(length, axis=1, keepdims=True)
+    spans_v[...] = jnp.where(lane == 0, first, length)
+    copy = pltpu.make_async_copy(spans_v, spans_s, sem)
+    copy.start()
+    copy.wait()
+
     lane = iota(1)
     row = iota(0)
 
     def body(o, carry):
-        start = start_ref[o]
-        base = pl.multiple_of((start // 128) * 128, 128)
-        window = w_ref[:, pl.ds(base, 256)]
-        window = pltpu.roll(window, 256 - (start - base), 1)[:, :128]
-        window = jnp.where((row == 0) & (lane >= len_ref[o]), 0.0, window)
+        start = spans_s[o, 0] & (PAR_DEV - 1)
+        tile = lax.div(start, 128)
+        first, second = w[tile], w[tile + 1]
+        offset = jnp.full((8, 128), start, jnp.int32)
+        ahead = pltpu.roll(jnp.where(lane < 64, second, first), 64, 1)
+        window = jnp.where((offset & 64) != 0, ahead, first)
+        for bit in (32, 16, 8, 4, 2, 1):
+            window = jnp.where((offset & bit) != 0, pltpu.roll(window, 128 - bit, 1), window)
+        window = jnp.where((row == 0) & (lane >= spans_s[o, 1]), 0.0, window)
         low = window[0:4]
         high = pltpu.roll(window, 64, 1)[4:8]
-        out_ref[o % N_CROSS, o // N_CROSS] = jnp.where(lane[0:4] < 64, low, high)
-        return carry
-
-    lax.fori_loop(0, N_SLAB * N_CROSS, body, 0, unroll=4)
-
-
-def pack(start, length, w):
-    return pl.pallas_call(
-        pack_kernel,
-        out_shape=jax.ShapeDtypeStruct((N_CROSS, N_SLAB, 4, 128), F32),
-        in_specs=[
-            pl.BlockSpec(memory_space=pltpu.SMEM),
-            pl.BlockSpec(memory_space=pltpu.SMEM),
-            pl.BlockSpec(memory_space=pltpu.VMEM),
-        ],
-        out_specs=pl.BlockSpec(memory_space=pltpu.VMEM),
-    )(start, length, w)
-
-
-def mix_kernel(*refs):
-    (s_ref, v_ref, h_ref, tg_ref, sb_ref) = refs[:5]
+        out[o % N_CROSS, o // N_CROSS] = jnp.where(lane[0:4] < 64, low, high)
+        return carry
+
+    lax.fori_loop(0, N_SLAB * N_CROSS, body, 0, unroll=8)
+
+
+def step_kernel(
+    s_ref, v_ref, h_ref, d_ref, tg_ref, mass_ref, ps_ref, box_ref, cell_ref, count_ref,
+    new_ref, tend_ref,
+    *scratch,
+):
     arrays = (s_ref, v_ref, h_ref)
-    placed = refs[5:9]
-    (xl, xh, zl, zh, z0, z15, r2) = refs[9:16]
-    bufs = refs[16:20]
-    outs = refs[20:24]
-    (tgb, inv_v, inv_s, r1) = refs[24:28]
-    (tsem, p1, p2, hsem, psem, lsem) = refs[28:34]
+    bufs = scratch[0:4]
+    outs = scratch[4:8]
+    placed = scratch[8:12]
+    (xl, xh, zl, zh, z0, z15) = scratch[12:18]
+    (sb, r1, r2) = scratch[18:21]
+    (tgv, tgb, inv_v, inv_s, w, spans_v, spans_s) = scratch[21:28]
+    (gx, hx, gy, hy, gz, hz, gzp, hzp, vals, tabs) = scratch[28:38]
+    (tsem, p1, p2, hsem, psem, lsem) = scratch[38:44]
 
     me_s = lax.axis_index("slab")
     me_c = lax.axis_index("cross")
@@ -123,12 +158,17 @@
     def drain(ref, sem):
         pltpu.make_async_copy(ref, ref, sem).wait()
 
+    mine = jnp.zeros((8, 128), jnp.int32)
+    for k in range(4):
+        mine = mine + jnp.where(iota(1) == 4 * me_c + k, tg_ref[0, k], 0)
+    tgv[...] = mine
+    tgb[me_c] = mine
+
     def send_targets(d, carry):
-        remote(tg_ref, tgb.at[me_c], tsem, (me_s, cross(d))).start()
+        remote(tgv, tgb.at[me_c], tsem, (me_s, cross(d))).start()
         return carry
 
     lax.fori_loop(1, N_CROSS, send_targets, 0)
-    tgb[me_c] = tg_ref[...]
 
     def parts(g):
         at = 0
@@ -190,27 +230,29 @@
     phase1(0)
     phase1(1)
 
+    pack(mass_ref, ps_ref, box_ref, cell_ref, count_ref, w, spans_v, spans_s, lsem.at[4], sb)
+
+    def parcels1(d, carry):
+        c = cross(d)
+        remote(sb.at[c], r1.at[me_c], psem.at[0], (me_s, c)).start()
+        return carry
+
+    lax.fori_loop(1, N_CROSS, parcels1, 0)
+
     drain(tgb.at[pl.ds(0, N_CROSS - 1)], tsem.at[1])
     flat = tgb[0]
     for s in range(1, N_CROSS):
         flat = flat + tgb[s]
     for tile in range(8):
         hit = flat == iota(0) + 8 * tile
-        code = jnp.sum(jnp.where(hit & (iota(1) < 64), iota(1).astype(F32), 0.0), axis=1, keepdims=True)
-        inv_v[8 * tile : 8 * tile + 8, :] = jnp.broadcast_to(code, (8, 128)).astype(jnp.int32)
+        code = jnp.sum(jnp.where(hit & (iota(1) < 64), iota(1), 0), axis=1, keepdims=True)
+        inv_v[8 * tile : 8 * tile + 8, :] = jnp.broadcast_to(code, (8, 128))
     to_scalar = pltpu.make_async_copy(inv_v, inv_s, lsem.at[4])
     to_scalar.start()
     to_scalar.wait()
 
     phase2(0)
-
-    def parcels1(d, carry):
-        c = cross(d)
-        remote(sb_ref.at[c], r1.at[me_c], psem.at[0], (me_s, c)).start()
-        return carry
-
-    lax.fori_loop(1, N_CROSS, parcels1, 0)
-    own = pltpu.make_async_copy(sb_ref.at[me_c], r1.at[me_c], lsem.at[4])
+    own = pltpu.make_async_copy(sb.at[me_c], r1.at[me_c], lsem.at[4])
     own.start()
     phase1(2)
     phase2(1)
@@ -234,9 +276,9 @@
     x_hi = (me_s, cross(1))
     halo = []
     for g in range(2):
-        at = pl.ds(sum(WIDTHS[:g]), WIDTHS[g])
-        halo.append(remote(placed[g].at[0], xh.at[at], hsem.at[g], x_lo))
-        halo.append(remote(placed[g].at[BE - 1], xl.at[at], hsem.at[2 + g], x_hi))
+        at, rows = pl.ds(sum(HALO[:g]), HALO[g]), pl.ds(0, HALO[g])
+        halo.append(remote(placed[g].at[0, rows], xh.at[at], hsem.at[g], x_lo))
+        halo.append(remote(placed[g].at[BE - 1, rows], xl.at[at], hsem.at[2 + g], x_hi))
     for copy in halo:
         copy.start()
     pack_z(placed, z0, z15)
@@ -247,13 +289,23 @@
         halo.append(copy)
 
     phase2(2)
-    phase2(3)
     for copy in halo:
         copy.wait()
+    transport(
+        d_ref, placed[0], placed[1], xl, xh, zl, zh, z0, z15, tend_ref,
+        gx, hx, gy, hy, gz, hz, gzp, hzp,
+    )
+    phase2(3)
+    advance(placed[0], 3, placed[1], 12, tend_ref, new_ref, 0, 1)
+    advance(placed[1], 11, placed[1], 13, tend_ref, new_ref, FIELDS - 1, 1)
     own.wait()
     drain(r2.at[pl.ds(0, N_SLAB - 1)], psem.at[1, 1])
+    deposit(placed[0], r2, new_ref, vals, tabs)
     landed(2)
+    advance(placed[0], 4, placed[2], 0, tend_ref, new_ref, 1, 9)
+    advance(placed[1], 0, placed[2], 9, tend_ref, new_ref, 10, 1)
     landed(3)
+    advance(placed[1], 1, placed[3], 0, tend_ref, new_ref, 11, 10)
 
     drain(tgb.at[pl.ds(0, N_CROSS - 1)], tsem.at[0])
     drain(r1.at[pl.ds(0, N_CROSS - 1)], psem.at[0, 0])
@@ -267,7 +319,7 @@
     upper = iota(0) >= 4
 
     for g in range(2):
-        first = sum(WIDTHS[:g])
+        first = sum(HALO[:g])
 
         def body(f, carry):
             low = [None, None]
@@ -286,26 +338,39 @@
             z15[first + f] = jnp.where(upper, high[1], sub_roll(high[0], 4))
             return carry
 
-        lax.fori_loop(0, WIDTHS[g], body, 0)
-
-
-def mix(state, velocity, history, targets, sendbuf):
+        lax.fori_loop(0, HALO[g], body, 0)
+
+
+def step(state, velocity, history, diffusion, targets, mass, parcels, box, cell, count):
     vm = pl.BlockSpec(memory_space=pltpu.VMEM)
+    sm = pl.BlockSpec(memory_space=pltpu.SMEM)
     hbm = pl.BlockSpec(memory_space=pl.ANY)
-    total = WIDTHS[0] + WIDTHS[1]
     group = [(N_CROSS, w, 8, 128) for w in WIDTHS]
-    outs = group + [(total, 8, 128)] * 6 + [(N_SLAB, N_CROSS, 4, 128)]
+    devices = N_SLAB * N_CROSS
+    out = jax.ShapeDtypeStruct((FIELDS, BE, 8, 128), F32)
     return pl.pallas_call(
-        mix_kernel,
-        out_shape=[jax.ShapeDtypeStruct(s, F32) for s in outs],
-        in_specs=[hbm, hbm, hbm, vm, vm],
-        out_specs=[vm] * len(outs),
-        scratch_shapes=[pltpu.VMEM(s, F32) for s in group + group]
+        step_kernel,
+        out_shape=[out, out],
+        in_specs=[hbm, hbm, hbm, sm, sm, vm, vm, vm, vm, sm],
+        out_specs=[vm, vm],
+        scratch_shapes=[pltpu.VMEM(s, F32) for s in group * 3]
+        + [pltpu.VMEM((sum(HALO), 8, 128), F32)] * 6
+        + [pltpu.VMEM((N_CROSS, N_SLAB, 4, 128), F32)] * 2
+        + [pltpu.VMEM((N_SLAB, N_CROSS, 4, 128), F32)]
         + [
+            pltpu.VMEM((8, 128), jnp.int32),
             pltpu.VMEM((N_CROSS, 8, 128), jnp.int32),
             pltpu.VMEM((64, 128), jnp.int32),
             pltpu.SMEM((64, 128), jnp.int32),
-            pltpu.VMEM((N_CROSS, N_SLAB, 4, 128), F32),
+            pltpu.VMEM((PAR_DEV // 128 + 1, 8, 128), F32),
+            pltpu.VMEM((devices, 128), jnp.int32),
+            pltpu.SMEM((devices, 128), jnp.int32),
+        ]
+        + [pltpu.VMEM((BE + 1, 8, 128), F32)] * 2
+        + [pltpu.VMEM((BE, 8, 128), F32)] * 4
+        + [pltpu.VMEM((2, 8, 128), F32)] * 2
+        + [pltpu.VMEM((8, devices * CAP), F32), pltpu.VMEM((640, 256), BF16)]
+        + [
             pltpu.SemaphoreType.DMA((2,)),
             pltpu.SemaphoreType.DMA((4, 2)),
             pltpu.SemaphoreType.DMA((4, 2)),
@@ -314,18 +379,17 @@
             pltpu.SemaphoreType.DMA((5,)),
         ],
         compiler_params=pltpu.CompilerParams(
-            collective_id=0, has_side_effects=True, vmem_limit_bytes=40 * 2**20
+            collective_id=0, has_side_effects=True, vmem_limit_bytes=VMEM_LIMIT
         ),
-    )(state, velocity, history, targets, sendbuf)
+    )(state, velocity, history, diffusion, targets, mass, parcels, box, cell, count)
 
 
 def spread_of(e):
     return 1.0 + 0.5 * jnp.tanh(e)
 
 
-def finish_kernel(
-    d_ref, p0, p1, p2, p3, xl, xh, zl, zh, z0, z15, r2, new_ref, tend_ref,
-    gx, hx, gy, hy, gz, hz, gzp, hzp, vals, tabs,
+def transport(
+    d_ref, p0, p1, xl, xh, zl, zh, z0, z15, tend_ref, gx, hx, gy, hy, gz, hz, gzp, hzp
 ):
     me_c = lax.axis_index("cross")
     lane = iota(1)
@@ -358,8 +422,8 @@
         ih, il = divmod(i, 8)
         return lane_roll(packed[ih], -16 * il)
 
-    E = WIDTHS[1] - 1
-    EH = WIDTHS[0] + WIDTHS[1] - 1
+    E = HALO[1] - 1
+    EH = HALO[0] + HALO[1] - 1
     first_wall = jnp.where(me_c == 0, 0.0, 1.0)
     last_wall = jnp.where(me_c == N_CROSS - 1, 0.0, 1.0)
     before_g = spread_of(xl[EH])
@@ -390,7 +454,7 @@
     def flux(d, g, h, low, high):
         return (d * g) * (high - low) - h * (high + low)
 
-    def transport(q_ref, h_ref, q_at, x_at, h_at, out_at, count):
+    def sweep(q_ref, q_at, x_at, out_at, count):
         def body(n, carry):
             f = out_at + n
             d = d_ref[f]
@@ -413,18 +477,27 @@
                 fy = flux(d, gy[i], hy[i], q, up_y(q))
                 total = total + fy - down_y(fy)
                 tend_ref[f, i] = total
-                old = h_ref[i, h_at + n]
-                new_ref[f, i] = q + TIME_STEP * (1.5 * total - 0.5 * old)
                 fx = fx_up
                 q = ahead
             return carry
 
         lax.fori_loop(0, count, body, 0)
 
-    transport(p0, p2, 3, 3, 0, 0, 10)
-    transport(p1, p2, 0, 13, 10, 10, 1)
-    transport(p1, p3, 1, 14, 0, 11, 11)
-
+    sweep(p0, 3, 3, 0, 10)
+    sweep(p1, 0, 13, 10, 12)
+
+
+def advance(q_ref, q_at, h_ref, h_at, tend_ref, new_ref, f_at, count):
+    def body(n, carry):
+        new_ref[f_at + n] = q_ref[:, q_at + n] + TIME_STEP * (
+            1.5 * tend_ref[f_at + n] - 0.5 * h_ref[:, h_at + n]
+        )
+        return carry
+
+    lax.fori_loop(0, count, body, 0)
+
+
+def deposit(p0, r2, new_ref, vals, tabs):
     tables = [new_ref[0], new_ref[FIELDS - 1]] + [p0[:, d] for d in range(3)]
     for n, table in enumerate(tables):
         table = table.reshape(128, 128)
@@ -445,7 +518,7 @@
 
     number = lax.broadcasted_iota(jnp.int32, (128, CHUNK), 0).astype(F32)
 
-    def deposit(n, acc):
+    def add_chunk(n, acc):
         v = vals[:, pl.ds(pl.multiple_of(n * CHUNK, CHUNK), CHUNK)]
         at_row = number == v[3:4]
         at_lane = jnp.where(number == v[7:8], 1.0, 0.0).astype(BF16)
@@ -475,31 +548,12 @@
         )
 
     acc = lax.fori_loop(
-        0, N_SLAB * N_CROSS * CAP // CHUNK, deposit, jnp.zeros((512, 128), F32)
+        0, N_SLAB * N_CROSS * CAP // CHUNK, add_chunk, jnp.zeros((512, 128), F32)
     )
     fuel = (acc[0:128] + acc[128:256]).reshape(BE, 8, 128)
     heat = (acc[256:384] + acc[384:512]).reshape(BE, 8, 128)
     new_ref[0] = new_ref[0] + DEPOSIT * fuel
     new_ref[FIELDS - 1] = new_ref[FIELDS - 1] + DEPOSIT * heat
-
-
-def finish(diffusion, arrived):
-    vm = pl.BlockSpec(memory_space=pltpu.VMEM)
-    out = jax.ShapeDtypeStruct((FIELDS, BE, 8, 128), F32)
-    return pl.pallas_call(
-        finish_kernel,
-        out_shape=[out, out],
-        in_specs=[pl.BlockSpec(memory_space=pltpu.SMEM)] + [vm] * len(arrived),
-        out_specs=[vm, vm],
-        scratch_shapes=[pltpu.VMEM((BE + 1, 8, 128), F32)] * 2
-        + [pltpu.VMEM((BE, 8, 128), F32)] * 4
-        + [pltpu.VMEM((2, 8, 128), F32)] * 2
-        + [
-            pltpu.VMEM((8, N_SLAB * N_CROSS * CAP), F32),
-            pltpu.VMEM((640, 256), BF16),
-        ],
-        compiler_params=pltpu.CompilerParams(vmem_limit_bytes=40 * 2**20),
-    )(diffusion, *arrived)
 
 
 def to_tiles(array):
@@ -526,27 +580,18 @@
     parcel_cell,
     parcel_count,
 ):
-    position = jnp.arange(PAR_DEV, dtype=jnp.int32)
-    owner = parcel_box // 4
-    here = owner[None, :] == jnp.arange(N_SLAB * N_CROSS, dtype=jnp.int32)[:, None]
-    start = jnp.min(jnp.where(here, position[None, :], PAR_DEV - 1), axis=1)
-    length = jnp.sum((here & (position < parcel_count[0])[None, :]).astype(jnp.int32), axis=1)
-    row = ((parcel_cell // 128) * 4 + parcel_box % 4).astype(F32)
-    lane = (parcel_cell % 128).astype(F32)
-    w = jnp.concatenate(
-        [parcel_mass[None], parcel_state[0:2], row[None], parcel_state[2:5], lane[None]], axis=0
+    new_state, tendency = step(
+        to_tiles(state),
+        to_tiles(velocity),
+        to_tiles(history),
+        diffusion,
+        box_target,
+        parcel_mass[None],
+        parcel_state,
+        parcel_box[None],
+        parcel_cell[None],
+        parcel_count,
     )
-    w = jnp.pad(w, ((0, 0), (0, 256)))
-    sendbuf = pack(start, length, w)
-
-    spot = jnp.arange(128, dtype=jnp.int32) - 4 * lax.axis_index("cross")
-    targets = jnp.sum(
-        jnp.where(spot[None, :] == jnp.arange(4, dtype=jnp.int32)[:, None], box_target[0][:, None], 0),
-        axis=0,
-    )
-    targets = jnp.broadcast_to(targets[None, :], (8, 128))
-    arrived = mix(to_tiles(state), to_tiles(velocity), to_tiles(history), targets, sendbuf)
-    new_state, tendency = finish(diffusion, arrived)
     return from_tiles(new_state), from_tiles(tendency)
 
 

time: 131 us -> 110 us (0.84)
  the two profiles are of different devices: /device:TPU:104 before, /device:TPU:1 now
where the time goes in v2:
time: 110 us; the launch traced here: 108 us
  Pallas kernels  103 us (94%)
  local copies, waits for them, and re-layouts  3.83 us (3%)
  between operations  1.3 us (1%)
    pallas_call x1, Pallas kernels, step(): pl.pallas_call(step_kernel, out_shape=[out, out], in_specs=[hbm, hbm, hbm...  103 us
    unnamed x4, local copies, waits for them, and re-layouts  3.83 us

profile of v2, /device:TPU:1, one launch (start us, length us, event | category | flops | bytes accessed | tf_op | source)
XLA Modules:
  0.0 108.1 jit_solution(2135326973050579410)
XLA Ops:
  1.3 103.0 %shard_map.113 = (f32[22,16,8,128]{3,2,1,0:T(8,128)}, f32[22,16,8,128]{3,2,1,0:T(8,128)}) custom-call(f32[22,16,8,128]{3,2,1,0:T(8,128)} %bitcast.28, f32[3,16,8,128]{3,2,1,0:T(8,128)} %bitcast.32, f32[22,16,8,128]{3,2,1,0:T(8,128)} %bitcast.29, f32[22]{0:T(128)} %d_ref.1, s32[1,4]{1,0:T(1,128)} %tg_ref.1, f32[1,4096]{1,0:T(1,128)} %bitcast.33, ...), custom_call_target="tpu_custom_call" | custom-call | tf_op jit(solution)/shard_map/pallas_call | solution.py:351
  104.3 0.0 copy-start
  104.3 2.7 %copy.20 = f32[22,4,4096]{2,1,0:T(4,128)} copy(f32[22,4,4096]{2,1,0:T(4,128)} %bitcast.31) | data formatting | bytes 2883584
  107.0 0.0 copy-done
  107.0 1.1 %copy.21 = f32[22,4,4096]{2,1,0:T(4,128)} copy(f32[22,4,4096]{2,1,0:T(4,128)S(1)} %bitcast.30) | data formatting | bytes 2883584
Async XLA Ops:
  104.3 2.7 %copy-start = (f32[22,16,8,128]{3,2,1,0:T(8,128)S(1)}, f32[22,16,8,128]{3,2,1,0:T(8,128)}, u32[]{:S(2)}) copy-start(f32[22,16,8,128]{3,2,1,0:T(8,128)} %get-tuple-element.5) | copy-start | bytes 4325380

commit v3 on v2

--- a/solution.py
+++ b/solution.py
@@ -125,8 +125,10 @@
     me_s = lax.axis_index("slab")
     me_c = lax.axis_index("cross")
 
+    me_x, me_z = lax.div(me_c, 4), lax.rem(me_c, 4)
+
     def cross(d):
-        return lax.rem(me_c + d, N_CROSS)
+        return lax.rem(me_x + lax.div(d, 4), 4) * 4 + lax.rem(me_z + lax.rem(d, 4), 4)
 
     def slab(d):
         return lax.rem(me_s + d, N_SLAB)
@@ -254,9 +256,7 @@
     phase2(0)
     own = pltpu.make_async_copy(sb.at[me_c], r1.at[me_c], lsem.at[4])
     own.start()
-    phase1(2)
     phase2(1)
-    phase1(3)
 
     own.wait()
     drain(r1.at[pl.ds(0, N_CROSS - 1)], psem.at[0, 1])
@@ -271,9 +271,10 @@
     own.start()
 
     landed(0)
+    phase1(2)
     landed(1)
-    x_lo = (me_s, cross(N_CROSS - 1))
-    x_hi = (me_s, cross(1))
+    x_lo = (me_s, lax.rem(me_c + N_CROSS - 1, N_CROSS))
+    x_hi = (me_s, lax.rem(me_c + 1, N_CROSS))
     halo = []
     for g in range(2):
         at, rows = pl.ds(sum(HALO[:g]), HALO[g]), pl.ds(0, HALO[g])
@@ -288,6 +289,7 @@
         copy.start()
         halo.append(copy)
 
+    phase1(3)
     phase2(2)
     for copy in halo:
         copy.wait()

time: 110 us -> 98.4 us (0.89)
  the two profiles are of different devices: /device:TPU:1 before, /device:TPU:52 now
where the time goes in v3:
time: 98.4 us; the launch traced here: 98.2 us
  Pallas kernels  93.1 us (95%)
  local copies, waits for them, and re-layouts  3.83 us (4%)
  between operations  1.3 us (1%)
    pallas_call x1, Pallas kernels, step(): pl.pallas_call(step_kernel, out_shape=[out, out], in_specs=[hbm, hbm, hbm...  93.1 us
    unnamed x4, local copies, waits for them, and re-layouts  3.83 us

profile of v3, /device:TPU:52, one launch (start us, length us, event | category | flops | bytes accessed | tf_op | source)
XLA Modules:
  0.0 98.2 jit_solution(13829016092257006532)
XLA Ops:
  1.3 93.1 %shard_map.113 = (f32[22,16,8,128]{3,2,1,0:T(8,128)}, f32[22,16,8,128]{3,2,1,0:T(8,128)}) custom-call(f32[22,16,8,128]{3,2,1,0:T(8,128)} %bitcast.28, f32[3,16,8,128]{3,2,1,0:T(8,128)} %bitcast.32, f32[22,16,8,128]{3,2,1,0:T(8,128)} %bitcast.29, f32[22]{0:T(128)} %d_ref.1, s32[1,4]{1,0:T(1,128)} %tg_ref.1, f32[1,4096]{1,0:T(1,128)} %bitcast.33, ...), custom_call_target="tpu_custom_call" | custom-call | tf_op jit(solution)/shard_map/pallas_call | solution.py:353
  94.4 0.0 copy-start
  94.4 2.7 %copy.20 = f32[22,4,4096]{2,1,0:T(4,128)} copy(f32[22,4,4096]{2,1,0:T(4,128)} %bitcast.31) | data formatting | bytes 2883584
  97.1 0.0 copy-done
  97.1 1.1 %copy.21 = f32[22,4,4096]{2,1,0:T(4,128)} copy(f32[22,4,4096]{2,1,0:T(4,128)S(1)} %bitcast.30) | data formatting | bytes 2883584
Async XLA Ops:
  94.4 2.7 %copy-start = (f32[22,16,8,128]{3,2,1,0:T(8,128)S(1)}, f32[22,16,8,128]{3,2,1,0:T(8,128)}, u32[]{:S(2)}) copy-start(f32[22,16,8,128]{3,2,1,0:T(8,128)} %get-tuple-element.5) | copy-start | bytes 4325380

commit v4 on v3

--- a/solution.py
+++ b/solution.py
@@ -23,13 +23,45 @@
 DEPOSIT = 0.25
 
 GROUPS = (
-    ((1, 0, 3), (0, 0, 10)),
-    ((0, 10, 12), (2, 0, 1), (2, 21, 1)),
-    ((2, 1, 10),),
-    ((2, 11, 10),),
+    ((1, 0, 3), (0, 0, 4)),
+    ((0, 4, 6),),
+    ((0, 10, 6),),
+    ((0, 16, 6), (2, 0, 1), (2, 21, 1)),
+    ((2, 1, 5),),
+    ((2, 6, 5),),
+    ((2, 11, 5),),
+    ((2, 16, 5),),
 )
-WIDTHS = (13, 14, 10, 10)
-HALO = (13, 12)
+WIDTHS = tuple(sum(part[2] for part in group) for group in GROUPS)
+N_GAS = 4
+GAS = tuple(sum(part[2] for part in group if part[0] < 2) for group in GROUPS[:N_GAS])
+
+SCHEDULE = (
+    ("1", 0), ("1", 1), ("1", 2), ("1", 3),
+    ("pack", 0), ("invert", 0),
+    ("2", 0), ("2", 1), ("2", 2), ("2", 3), ("pass", 0),
+    ("landed", 0), ("landed", 1), ("1", 4), ("landed", 2), ("landed", 3),
+    ("halo", 0), ("1", 5), ("1", 6), ("1", 7), ("faces", 0), ("sweep", 0), ("sweep", 1), ("sweep", 2), ("sweep", 3), ("2", 4), ("2", 5), ("2", 6), ("2", 7),
+    ("advance", 3), ("parcels", 0), ("chunks", 0), ("chunks", 1), ("chunks", 2), ("chunks", 3), ("deposit", 0),
+    ("landed", 4), ("advance", 4), ("landed", 5), ("advance", 5), ("landed", 6), ("advance", 6), ("landed", 7), ("advance", 7),
+)
+
+
+def runs(which):
+    found = []
+    for g, group in enumerate(GROUPS):
+        row = 0
+        for source, first, count in group:
+            if source == which:
+                found.append((first, count, g, row))
+            row += count
+    return sorted(found)
+
+
+def place_of(which, field):
+    for first, count, g, row in runs(which):
+        if first <= field < first + count:
+            return g, row + field - first, first + count - field
 
 
 def iota(dim, shape=(8, 128)):
@@ -109,18 +141,19 @@
 
 def step_kernel(
     s_ref, v_ref, h_ref, d_ref, tg_ref, mass_ref, ps_ref, box_ref, cell_ref, count_ref,
-    new_ref, tend_ref,
+    new_out, tend_out,
     *scratch,
 ):
     arrays = (s_ref, v_ref, h_ref)
-    bufs = scratch[0:4]
-    outs = scratch[4:8]
-    placed = scratch[8:12]
-    (xl, xh, zl, zh, z0, z15) = scratch[12:18]
-    (sb, r1, r2) = scratch[18:21]
-    (tgv, tgb, inv_v, inv_s, w, spans_v, spans_s) = scratch[21:28]
-    (gx, hx, gy, hy, gz, hz, gzp, hzp, vals, tabs) = scratch[28:38]
-    (tsem, p1, p2, hsem, psem, lsem) = scratch[38:44]
+    n = len(GROUPS)
+    bufs, outs, placed = scratch[0:n], scratch[n : 2 * n], scratch[2 * n : 3 * n]
+    scratch = scratch[3 * n :]
+    (xl, xh, zl, zh, z0, z15) = scratch[0:6]
+    (sb, r1, r2) = scratch[6:9]
+    (tgv, tgb, inv_v, inv_s, w, spans_v, spans_s) = scratch[9:16]
+    (gx, hx, gy, hy, gz, hz, gzp, hzp, vals, tabs) = scratch[16:26]
+    (tsem, p1, p2, hsem, psem, lsem) = scratch[26:32]
+    (new_ref, tend_ref, osem) = scratch[32:35]
 
     me_s = lax.axis_index("slab")
     me_c = lax.axis_index("cross")
@@ -229,90 +262,116 @@
         drain(bufs[g].at[pl.ds(0, N_CROSS - 1)], p1.at[g, 0])
         drain(outs[g].at[pl.ds(0, N_CROSS - 1)], p2.at[g, 0])
 
-    phase1(0)
-    phase1(1)
-
-    pack(mass_ref, ps_ref, box_ref, cell_ref, count_ref, w, spans_v, spans_s, lsem.at[4], sb)
+    def invert():
+        drain(tgb.at[pl.ds(0, N_CROSS - 1)], tsem.at[1])
+        flat = tgb[0]
+        for s in range(1, N_CROSS):
+            flat = flat + tgb[s]
+        for tile in range(8):
+            hit = flat == iota(0) + 8 * tile
+            code = jnp.sum(jnp.where(hit & (iota(1) < 64), iota(1), 0), axis=1, keepdims=True)
+            inv_v[8 * tile : 8 * tile + 8, :] = jnp.broadcast_to(code, (8, 128))
+        to_scalar = pltpu.make_async_copy(inv_v, inv_s, lsem.at[n])
+        to_scalar.start()
+        to_scalar.wait()
+
+    halo = []
+
+    def send_halos():
+        x_lo = (me_s, lax.rem(me_c + N_CROSS - 1, N_CROSS))
+        x_hi = (me_s, lax.rem(me_c + 1, N_CROSS))
+        for g in range(N_GAS):
+            at = pl.ds(sum(GAS[:g]), GAS[g])
+            rows = pl.ds(0, GAS[g])
+            halo.append(remote(placed[g].at[0, rows], xh.at[at], hsem.at[2 * g], x_lo))
+            halo.append(remote(placed[g].at[BE - 1, rows], xl.at[at], hsem.at[2 * g + 1], x_hi))
+        for copy in halo:
+            copy.start()
+        pack_z(placed, z0, z15)
+        z_lo = (slab(N_SLAB - 1), me_c)
+        z_hi = (slab(1), me_c)
+        for copy in (
+            remote(z0, zh, hsem.at[2 * N_GAS], z_lo),
+            remote(z15, zl, hsem.at[2 * N_GAS + 1], z_hi),
+        ):
+            copy.start()
+            halo.append(copy)
 
     def parcels1(d, carry):
         c = cross(d)
         remote(sb.at[c], r1.at[me_c], psem.at[0], (me_s, c)).start()
         return carry
 
-    lax.fori_loop(1, N_CROSS, parcels1, 0)
-
-    drain(tgb.at[pl.ds(0, N_CROSS - 1)], tsem.at[1])
-    flat = tgb[0]
-    for s in range(1, N_CROSS):
-        flat = flat + tgb[s]
-    for tile in range(8):
-        hit = flat == iota(0) + 8 * tile
-        code = jnp.sum(jnp.where(hit & (iota(1) < 64), iota(1), 0), axis=1, keepdims=True)
-        inv_v[8 * tile : 8 * tile + 8, :] = jnp.broadcast_to(code, (8, 128))
-    to_scalar = pltpu.make_async_copy(inv_v, inv_s, lsem.at[4])
-    to_scalar.start()
-    to_scalar.wait()
-
-    phase2(0)
-    own = pltpu.make_async_copy(sb.at[me_c], r1.at[me_c], lsem.at[4])
-    own.start()
-    phase2(1)
-
-    own.wait()
-    drain(r1.at[pl.ds(0, N_CROSS - 1)], psem.at[0, 1])
-
     def parcels2(d, carry):
         a = slab(d)
         remote(r1.at[:, a], r2.at[me_s], psem.at[1], (a, me_c)).start()
         return carry
 
-    lax.fori_loop(1, N_SLAB, parcels2, 0)
-    own = pltpu.make_async_copy(r1.at[:, me_s], r2.at[me_s], lsem.at[4])
-    own.start()
-
-    landed(0)
-    phase1(2)
-    landed(1)
-    x_lo = (me_s, lax.rem(me_c + N_CROSS - 1, N_CROSS))
-    x_hi = (me_s, lax.rem(me_c + 1, N_CROSS))
-    halo = []
-    for g in range(2):
-        at, rows = pl.ds(sum(HALO[:g]), HALO[g]), pl.ds(0, HALO[g])
-        halo.append(remote(placed[g].at[0, rows], xh.at[at], hsem.at[g], x_lo))
-        halo.append(remote(placed[g].at[BE - 1, rows], xl.at[at], hsem.at[2 + g], x_hi))
-    for copy in halo:
-        copy.start()
-    pack_z(placed, z0, z15)
-    z_lo = (slab(N_SLAB - 1), me_c)
-    z_hi = (slab(1), me_c)
-    for copy in (remote(z0, zh, hsem.at[4], z_lo), remote(z15, zl, hsem.at[5], z_hi)):
-        copy.start()
-        halo.append(copy)
-
-    phase1(3)
-    phase2(2)
-    for copy in halo:
-        copy.wait()
-    transport(
-        d_ref, placed[0], placed[1], xl, xh, zl, zh, z0, z15, tend_ref,
-        gx, hx, gy, hy, gz, hz, gzp, hzp,
-    )
-    phase2(3)
-    advance(placed[0], 3, placed[1], 12, tend_ref, new_ref, 0, 1)
-    advance(placed[1], 11, placed[1], 13, tend_ref, new_ref, FIELDS - 1, 1)
-    own.wait()
-    drain(r2.at[pl.ds(0, N_SLAB - 1)], psem.at[1, 1])
-    deposit(placed[0], r2, new_ref, vals, tabs)
-    landed(2)
-    advance(placed[0], 4, placed[2], 0, tend_ref, new_ref, 1, 9)
-    advance(placed[1], 0, placed[2], 9, tend_ref, new_ref, 10, 1)
-    landed(3)
-    advance(placed[1], 1, placed[3], 0, tend_ref, new_ref, 11, 10)
-
+    kept = {}
+
+    def write(ref, out, sem, first, count):
+        at = pl.ds(first, count)
+        pltpu.make_async_copy(ref.at[at], out.at[at], sem).start()
+
+    chunks = N_SLAB * N_CROSS * CAP // CHUNK
+    for name, g in SCHEDULE:
+        if name == "1":
+            phase1(g)
+        elif name == "2":
+            phase2(g)
+        elif name == "landed":
+            landed(g)
+        elif name == "pack":
+            pack(mass_ref, ps_ref, box_ref, cell_ref, count_ref, w, spans_v, spans_s, lsem.at[n], sb)
+            lax.fori_loop(1, N_CROSS, parcels1, 0)
+            own = pltpu.make_async_copy(sb.at[me_c], r1.at[me_c], lsem.at[n])
+            own.start()
+            own.wait()
+        elif name == "invert":
+            invert()
+        elif name == "pass":
+            drain(r1.at[pl.ds(0, N_CROSS - 1)], psem.at[0, 1])
+            lax.fori_loop(1, N_SLAB, parcels2, 0)
+            own = pltpu.make_async_copy(r1.at[:, me_s], r2.at[me_s], lsem.at[n])
+            own.start()
+            own.wait()
+        elif name == "halo":
+            send_halos()
+        elif name == "faces":
+            for copy in halo:
+                copy.wait()
+            kept["sweep"] = faces(
+                d_ref, placed, xl, xh, zl, zh, z0, z15, tend_ref,
+                gx, hx, gy, hy, gz, hz, gzp, hzp,
+            )
+        elif name == "sweep":
+            kept["sweep"](g)
+            for first, count, group, _ in runs(0):
+                if group == g:
+                    write(tend_ref, tend_out, osem.at[0], first, count)
+        elif name == "advance":
+            advance(placed, g, tend_ref, new_ref)
+            for first, count, group, _ in runs(2):
+                if group == g and first not in (0, FIELDS - 1):
+                    write(new_ref, new_out, osem.at[1], first, count)
+        elif name == "parcels":
+            drain(r2.at[pl.ds(0, N_SLAB - 1)], psem.at[1, 1])
+            deposit_start(placed[0], r2, new_ref, vals, tabs)
+            kept["acc"] = jnp.zeros((512, 128), F32)
+        elif name == "chunks":
+            low, high = chunks * g // 4, chunks * (g + 1) // 4
+            kept["acc"] = deposit_chunks(low, high, kept["acc"], vals, tabs)
+        elif name == "deposit":
+            deposit_end(kept["acc"], new_ref)
+            write(new_ref, new_out, osem.at[1], 0, 1)
+            write(new_ref, new_out, osem.at[1], FIELDS - 1, 1)
+
+    drain(tend_ref, osem.at[0])
+    drain(new_ref, osem.at[1])
     drain(tgb.at[pl.ds(0, N_CROSS - 1)], tsem.at[0])
     drain(r1.at[pl.ds(0, N_CROSS - 1)], psem.at[0, 0])
     drain(r2.at[pl.ds(0, N_SLAB - 1)], psem.at[1, 0])
-    for g in range(4):
+    for g in range(n):
         sent(g)
 
 
@@ -320,8 +379,8 @@
     lane16 = iota(1) // 16
     upper = iota(0) >= 4
 
-    for g in range(2):
-        first = sum(HALO[:g])
+    for g in range(N_GAS):
+        first = sum(GAS[:g])
 
         def body(f, carry):
             low = [None, None]
@@ -340,7 +399,7 @@
             z15[first + f] = jnp.where(upper, high[1], sub_roll(high[0], 4))
             return carry
 
-        lax.fori_loop(0, HALO[g], body, 0)
+        lax.fori_loop(0, GAS[g], body, 0)
 
 
 def step(state, velocity, history, diffusion, targets, mass, parcels, box, cell, count):
@@ -354,9 +413,9 @@
         step_kernel,
         out_shape=[out, out],
         in_specs=[hbm, hbm, hbm, sm, sm, vm, vm, vm, vm, sm],
-        out_specs=[vm, vm],
+        out_specs=[hbm, hbm],
         scratch_shapes=[pltpu.VMEM(s, F32) for s in group * 3]
-        + [pltpu.VMEM((sum(HALO), 8, 128), F32)] * 6
+        + [pltpu.VMEM((sum(GAS), 8, 128), F32)] * 6
         + [pltpu.VMEM((N_CROSS, N_SLAB, 4, 128), F32)] * 2
         + [pltpu.VMEM((N_SLAB, N_CROSS, 4, 128), F32)]
         + [
@@ -374,11 +433,14 @@
         + [pltpu.VMEM((8, devices * CAP), F32), pltpu.VMEM((640, 256), BF16)]
         + [
             pltpu.SemaphoreType.DMA((2,)),
-            pltpu.SemaphoreType.DMA((4, 2)),
-            pltpu.SemaphoreType.DMA((4, 2)),
-            pltpu.SemaphoreType.DMA((6, 2)),
+            pltpu.SemaphoreType.DMA((len(GROUPS), 2)),
+            pltpu.SemaphoreType.DMA((len(GROUPS), 2)),
+            pltpu.SemaphoreType.DMA((2 * N_GAS + 2, 2)),
             pltpu.SemaphoreType.DMA((2, 2)),
-            pltpu.SemaphoreType.DMA((5,)),
+            pltpu.SemaphoreType.DMA((len(GROUPS) + 1,)),
+            pltpu.VMEM((FIELDS, BE, 8, 128), F32),
+            pltpu.VMEM((FIELDS, BE, 8, 128), F32),
+            pltpu.SemaphoreType.DMA((2,)),
         ],
         compiler_params=pltpu.CompilerParams(
             collective_id=0, has_side_effects=True, vmem_limit_bytes=VMEM_LIMIT
@@ -386,12 +448,47 @@
     )(state, velocity, history, diffusion, targets, mass, parcels, box, cell, count)
 
 
+def hand_over_kernel(a_ref, b_ref, a_out, b_out, a_held, b_held, sems):
+    parts = 2
+    steps = []
+    for k, (src, held, dst) in enumerate(((a_ref, a_held, a_out), (b_ref, b_held, b_out))):
+        for part in range(parts):
+            at = pl.ds(part * (FIELDS // parts), FIELDS // parts)
+            steps.append(
+                (
+                    pltpu.make_async_copy(src.at[at], held.at[at], sems.at[0, parts * k + part]),
+                    pltpu.make_async_copy(held.at[at], dst.at[at], sems.at[1, parts * k + part]),
+                )
+            )
+    for fetch, _ in steps:
+        fetch.start()
+    for fetch, store in steps:
+        fetch.wait()
+        store.start()
+    for _, store in steps:
+        store.wait()
+
+
+def hand_over(a, b):
+    hbm = pl.BlockSpec(memory_space=pl.ANY)
+    out = jax.ShapeDtypeStruct((FIELDS, BE, 8, 128), F32)
+    return pl.pallas_call(
+        hand_over_kernel,
+        out_shape=[out, out],
+        in_specs=[hbm, hbm],
+        out_specs=[hbm, hbm],
+        scratch_shapes=[pltpu.VMEM((FIELDS, BE, 8, 128), F32)] * 2
+        + [pltpu.SemaphoreType.DMA((2, 4))],
+        compiler_params=pltpu.CompilerParams(vmem_limit_bytes=VMEM_LIMIT),
+    )(a, b)
+
+
 def spread_of(e):
     return 1.0 + 0.5 * jnp.tanh(e)
 
 
-def transport(
-    d_ref, p0, p1, xl, xh, zl, zh, z0, z15, tend_ref, gx, hx, gy, hy, gz, hz, gzp, hzp
+def faces(
+    d_ref, placed, xl, xh, zl, zh, z0, z15, tend_ref, gx, hx, gy, hy, gz, hz, gzp, hzp
 ):
     me_c = lax.axis_index("cross")
     lane = iota(1)
@@ -424,15 +521,17 @@
         ih, il = divmod(i, 8)
         return lane_roll(packed[ih], -16 * il)
 
-    E = HALO[1] - 1
-    EH = HALO[0] + HALO[1] - 1
+    p0 = placed[0]
+    pe, E, _ = place_of(0, FIELDS - 1)
+    EH = sum(GAS[:pe]) + E
+    pe = placed[pe]
     first_wall = jnp.where(me_c == 0, 0.0, 1.0)
     last_wall = jnp.where(me_c == N_CROSS - 1, 0.0, 1.0)
     before_g = spread_of(xl[EH])
     before_u = xl[0]
     for i in range(BE + 1):
         if i < BE:
-            now_g, now_u = spread_of(p1[i, E]), p0[i, 0]
+            now_g, now_u = spread_of(pe[i, E]), p0[i, 0]
         else:
             now_g, now_u = spread_of(xh[EH]), xh[0]
         g, h = 0.5 * (before_g + now_g), 0.25 * (before_u + now_u)
@@ -485,21 +584,37 @@
 
         lax.fori_loop(0, count, body, 0)
 
-    sweep(p0, 3, 3, 0, 10)
-    sweep(p1, 0, 13, 10, 12)
-
-
-def advance(q_ref, q_at, h_ref, h_at, tend_ref, new_ref, f_at, count):
-    def body(n, carry):
-        new_ref[f_at + n] = q_ref[:, q_at + n] + TIME_STEP * (
-            1.5 * tend_ref[f_at + n] - 0.5 * h_ref[:, h_at + n]
+    def sweep_group(g):
+        for first, count, group, row in runs(0):
+            if group == g:
+                sweep(placed[g], row, sum(GAS[:g]) + row, first, count)
+
+    return sweep_group
+
+
+def advance(placed, g, tend_ref, new_ref):
+    for first, count, group, h_row in runs(2):
+        if group != g:
+            continue
+        f = first
+        while f < first + count:
+            q_group, q_row, left = place_of(0, f)
+            many = min(left, first + count - f)
+            advance_run(placed[q_group], q_row, placed[g], h_row + f - first, tend_ref, new_ref, f, many)
+            f += many
+
+
+def advance_run(q_ref, q_at, h_ref, h_at, tend_ref, new_ref, f_at, count):
+    def body(m, carry):
+        new_ref[f_at + m] = q_ref[:, q_at + m] + TIME_STEP * (
+            1.5 * tend_ref[f_at + m] - 0.5 * h_ref[:, h_at + m]
         )
         return carry
 
     lax.fori_loop(0, count, body, 0)
 
 
-def deposit(p0, r2, new_ref, vals, tabs):
+def deposit_start(p0, r2, new_ref, vals, tabs):
     tables = [new_ref[0], new_ref[FIELDS - 1]] + [p0[:, d] for d in range(3)]
     for n, table in enumerate(tables):
         table = table.reshape(128, 128)
@@ -518,6 +633,8 @@
 
     lax.fori_loop(0, 64, unpack, 0, unroll=4)
 
+
+def deposit_chunks(low, high, acc, vals, tabs):
     number = lax.broadcasted_iota(jnp.int32, (128, CHUNK), 0).astype(F32)
 
     def add_chunk(n, acc):
@@ -549,9 +666,10 @@
             preferred_element_type=F32,
         )
 
-    acc = lax.fori_loop(
-        0, N_SLAB * N_CROSS * CAP // CHUNK, add_chunk, jnp.zeros((512, 128), F32)
-    )
+    return lax.fori_loop(low, high, add_chunk, acc)
+
+
+def deposit_end(acc, new_ref):
     fuel = (acc[0:128] + acc[128:256]).reshape(BE, 8, 128)
     heat = (acc[256:384] + acc[384:512]).reshape(BE, 8, 128)
     new_ref[0] = new_ref[0] + DEPOSIT * fuel
@@ -594,6 +712,7 @@
         parcel_cell[None],
         parcel_count,
     )
+    new_state, tendency = hand_over(new_state, tendency)
     return from_tiles(new_state), from_tiles(tendency)
 
 

time: 98.4 us -> 90.9 us (0.924)
  the two profiles are of different devices: /device:TPU:52 before, /device:TPU:1 now
where the time goes in v4:
time: 90.9 us; the launch traced here: 90.7 us
  Pallas kernels  89.4 us (98%)
  between operations  1.29 us (1%)
    pallas_call x1, Pallas kernels, step(): pl.pallas_call(step_kernel, out_shape=[out, out], in_specs=[hbm, hbm, hbm...  86.7 us
    pallas_call x1, Pallas kernels, hand_over(): pl.pallas_call(hand_over_kernel, out_shape=[out, out], in_specs=[hbm, hbm...  2.75 us

profile of v4, /device:TPU:1, one launch (start us, length us, event | category | flops | bytes accessed | tf_op | source)
XLA Modules:
  0.0 90.7 jit_solution(6073352142688878673)
XLA Ops:
  1.3 86.7 %shard_map.113 = (f32[22,16,8,128]{3,2,1,0:T(8,128)}, f32[22,16,8,128]{3,2,1,0:T(8,128)}) custom-call(f32[22,16,8,128]{3,2,1,0:T(8,128)} %bitcast.28, f32[3,16,8,128]{3,2,1,0:T(8,128)} %bitcast.30, f32[22,16,8,128]{3,2,1,0:T(8,128)} %bitcast.29, f32[22]{0:T(128)} %d_ref.1, s32[1,4]{1,0:T(1,128)} %tg_ref.1, f32[1,4096]{1,0:T(1,128)} %bitcast.31, ...), custom_call_target="tpu_custom_call" | custom-call | tf_op jit(solution)/shard_map/pallas_call | solution.py:412
  88.0 2.7 %shard_map.114 = (f32[22,16,8,128]{3,2,1,0:T(8,128)}, f32[22,16,8,128]{3,2,1,0:T(8,128)}) custom-call(f32[22,16,8,128]{3,2,1,0:T(8,128)} %get-tuple-element.6.a_ref, f32[22,16,8,128]{3,2,1,0:T(8,128)} %get-tuple-element.7.b_ref), custom_call_target="tpu_custom_call" | custom-call | tf_op jit(solution)/shard_map/pallas_call | solution.py:475

commit v5 on v4

--- a/solution.py
+++ b/solution.py
@@ -16,7 +16,7 @@
 N_SLAB = 8
 N_CROSS = 16
 CHUNK = 512
-VMEM_LIMIT = 60 * 2**20
+VMEM_LIMIT = 54 * 2**20
 
 TIME_STEP = 0.2
 LATENT = 0.5
@@ -140,8 +140,8 @@
 
 
 def step_kernel(
-    s_ref, v_ref, h_ref, d_ref, tg_ref, mass_ref, ps_ref, box_ref, cell_ref, count_ref,
-    new_out, tend_out,
+    s_ref, v_ref, h_ref, d_ref, tg_ref, mass_hbm, ps_hbm, box_hbm, cell_hbm, count_ref,
+    new_ref, tend_ref,
     *scratch,
 ):
     arrays = (s_ref, v_ref, h_ref)
@@ -153,7 +153,21 @@
     (tgv, tgb, inv_v, inv_s, w, spans_v, spans_s) = scratch[9:16]
     (gx, hx, gy, hy, gz, hz, gzp, hzp, vals, tabs) = scratch[16:26]
     (tsem, p1, p2, hsem, psem, lsem) = scratch[26:32]
-    (new_ref, tend_ref, osem) = scratch[32:35]
+    (mass_ref, ps_ref, box_ref, cell_ref, isem) = scratch[32:37]
+
+    fetches = [
+        pltpu.make_async_copy(src, dst, isem.at[k])
+        for k, (src, dst) in enumerate(
+            (
+                (mass_hbm, mass_ref),
+                (ps_hbm, ps_ref),
+                (box_hbm, box_ref),
+                (cell_hbm, cell_ref),
+            )
+        )
+    ]
+    for fetch in fetches:
+        fetch.start()
 
     me_s = lax.axis_index("slab")
     me_c = lax.axis_index("cross")
@@ -308,11 +322,6 @@
         return carry
 
     kept = {}
-
-    def write(ref, out, sem, first, count):
-        at = pl.ds(first, count)
-        pltpu.make_async_copy(ref.at[at], out.at[at], sem).start()
-
     chunks = N_SLAB * N_CROSS * CAP // CHUNK
     for name, g in SCHEDULE:
         if name == "1":
@@ -322,6 +331,8 @@
         elif name == "landed":
             landed(g)
         elif name == "pack":
+            for fetch in fetches:
+                fetch.wait()
             pack(mass_ref, ps_ref, box_ref, cell_ref, count_ref, w, spans_v, spans_s, lsem.at[n], sb)
             lax.fori_loop(1, N_CROSS, parcels1, 0)
             own = pltpu.make_async_copy(sb.at[me_c], r1.at[me_c], lsem.at[n])
@@ -346,14 +357,8 @@
             )
         elif name == "sweep":
             kept["sweep"](g)
-            for first, count, group, _ in runs(0):
-                if group == g:
-                    write(tend_ref, tend_out, osem.at[0], first, count)
         elif name == "advance":
             advance(placed, g, tend_ref, new_ref)
-            for first, count, group, _ in runs(2):
-                if group == g and first not in (0, FIELDS - 1):
-                    write(new_ref, new_out, osem.at[1], first, count)
         elif name == "parcels":
             drain(r2.at[pl.ds(0, N_SLAB - 1)], psem.at[1, 1])
             deposit_start(placed[0], r2, new_ref, vals, tabs)
@@ -363,11 +368,7 @@
             kept["acc"] = deposit_chunks(low, high, kept["acc"], vals, tabs)
         elif name == "deposit":
             deposit_end(kept["acc"], new_ref)
-            write(new_ref, new_out, osem.at[1], 0, 1)
-            write(new_ref, new_out, osem.at[1], FIELDS - 1, 1)
-
-    drain(tend_ref, osem.at[0])
-    drain(new_ref, osem.at[1])
+
     drain(tgb.at[pl.ds(0, N_CROSS - 1)], tsem.at[0])
     drain(r1.at[pl.ds(0, N_CROSS - 1)], psem.at[0, 0])
     drain(r2.at[pl.ds(0, N_SLAB - 1)], psem.at[1, 0])
@@ -411,9 +412,9 @@
     out = jax.ShapeDtypeStruct((FIELDS, BE, 8, 128), F32)
     return pl.pallas_call(
         step_kernel,
-        out_shape=[out, out],
-        in_specs=[hbm, hbm, hbm, sm, sm, vm, vm, vm, vm, sm],
-        out_specs=[hbm, hbm],
+        out_shape=[pltpu.VMEM((FIELDS, BE, 8, 128), F32)] * 2,
+        in_specs=[hbm, hbm, hbm, sm, sm, hbm, hbm, hbm, hbm, sm],
+        out_specs=[vm, vm],
         scratch_shapes=[pltpu.VMEM(s, F32) for s in group * 3]
         + [pltpu.VMEM((sum(GAS), 8, 128), F32)] * 6
         + [pltpu.VMEM((N_CROSS, N_SLAB, 4, 128), F32)] * 2
@@ -438,9 +439,11 @@
             pltpu.SemaphoreType.DMA((2 * N_GAS + 2, 2)),
             pltpu.SemaphoreType.DMA((2, 2)),
             pltpu.SemaphoreType.DMA((len(GROUPS) + 1,)),
-            pltpu.VMEM((FIELDS, BE, 8, 128), F32),
-            pltpu.VMEM((FIELDS, BE, 8, 128), F32),
-            pltpu.SemaphoreType.DMA((2,)),
+            pltpu.VMEM((1, PAR_DEV), F32),
+            pltpu.VMEM((5, PAR_DEV), F32),
+            pltpu.VMEM((1, PAR_DEV), jnp.int32),
+            pltpu.VMEM((1, PAR_DEV), jnp.int32),
+            pltpu.SemaphoreType.DMA((4,)),
         ],
         compiler_params=pltpu.CompilerParams(
             collective_id=0, has_side_effects=True, vmem_limit_bytes=VMEM_LIMIT
@@ -448,38 +451,27 @@
     )(state, velocity, history, diffusion, targets, mass, parcels, box, cell, count)
 
 
-def hand_over_kernel(a_ref, b_ref, a_out, b_out, a_held, b_held, sems):
-    parts = 2
-    steps = []
-    for k, (src, held, dst) in enumerate(((a_ref, a_held, a_out), (b_ref, b_held, b_out))):
-        for part in range(parts):
-            at = pl.ds(part * (FIELDS // parts), FIELDS // parts)
-            steps.append(
-                (
-                    pltpu.make_async_copy(src.at[at], held.at[at], sems.at[0, parts * k + part]),
-                    pltpu.make_async_copy(held.at[at], dst.at[at], sems.at[1, parts * k + part]),
-                )
-            )
-    for fetch, _ in steps:
-        fetch.start()
-    for fetch, store in steps:
-        fetch.wait()
-        store.start()
-    for _, store in steps:
-        store.wait()
+def hand_over_kernel(a_ref, b_ref, a_out, b_out, sems):
+    copies = []
+    for k, (src, dst) in enumerate(((a_ref, a_out), (b_ref, b_out))):
+        for part in range(2):
+            at = pl.ds(part * (FIELDS // 2), FIELDS // 2)
+            copies.append(pltpu.make_async_copy(src.at[at], dst.at[at], sems.at[2 * k + part]))
+    for copy in copies:
+        copy.start()
+    for copy in copies:
+        copy.wait()
 
 
 def hand_over(a, b):
-    hbm = pl.BlockSpec(memory_space=pl.ANY)
     out = jax.ShapeDtypeStruct((FIELDS, BE, 8, 128), F32)
     return pl.pallas_call(
         hand_over_kernel,
         out_shape=[out, out],
-        in_specs=[hbm, hbm],
-        out_specs=[hbm, hbm],
-        scratch_shapes=[pltpu.VMEM((FIELDS, BE, 8, 128), F32)] * 2
-        + [pltpu.SemaphoreType.DMA((2, 4))],
-        compiler_params=pltpu.CompilerParams(vmem_limit_bytes=VMEM_LIMIT),
+        in_specs=[pl.BlockSpec(memory_space=pl.ANY)] * 2,
+        out_specs=[pl.BlockSpec(memory_space=pl.ANY)] * 2,
+        scratch_shapes=[pltpu.SemaphoreType.DMA((4,))],
+        compiler_params=pltpu.CompilerParams(vmem_limit_bytes=8 * 2**20),
     )(a, b)
 
 

time: 90.9 us -> 88.8 us (0.977)
  Pallas kernels: 89.4 us -> 87.3 us
    pallas_call x2, Pallas kernels: 89.4 us -> 87.3 us  [the longest x1 85.7 us: step(): pl.pallas_call(step_kernel, out_shape=[pltpu.VMEM((FIELDS, BE, 8, 128), F...]
where the time goes in v5:
time: 88.8 us; the launch traced here: 88.6 us
  Pallas kernels  87.3 us (98%)
  between operations  1.29 us (1%)
    pallas_call x1, Pallas kernels, step(): pl.pallas_call(step_kernel, out_shape=[pltpu.VMEM((FIELDS, BE, 8, 128), F...  85.7 us

profile of v5, /device:TPU:1, one launch (start us, length us, event | category | flops | bytes accessed | tf_op | source)
XLA Modules:
  0.0 88.6 jit_solution(2805910444752039019)
XLA Ops:
  1.3 85.7 %shard_map.113 = (f32[22,16,8,128]{3,2,1,0:T(8,128)S(1)}, f32[22,16,8,128]{3,2,1,0:T(8,128)S(1)}) custom-call(f32[22,16,8,128]{3,2,1,0:T(8,128)} %bitcast.28, f32[3,16,8,128]{3,2,1,0:T(8,128)} %bitcast.30, f32[22,16,8,128]{3,2,1,0:T(8,128)} %bitcast.29, f32[22]{0:T(128)} %d_ref.1, s32[1,4]{1,0:T(1,128)} %tg_ref.1, f32[1,4096]{1,0:T(1,128)} %bitcast.31, ...), custom_call_target="tpu_custom_call" | custom-call | tf_op jit(solution)/shard_map/pallas_call | solution.py:413
  87.0 1.6 %shard_map.114 = (f32[22,16,8,128]{3,2,1,0:T(8,128)}, f32[22,16,8,128]{3,2,1,0:T(8,128)}) custom-call(f32[22,16,8,128]{3,2,1,0:T(8,128)S(1)} %get-tuple-element.6.a_ref, f32[22,16,8,128]{3,2,1,0:T(8,128)S(1)} %get-tuple-element.7.b_ref), custom_call_target="tpu_custom_call" | custom-call | tf_op jit(solution)/shard_map/pallas_call | solution.py:468

commit v6 on v5

--- a/solution.py
+++ b/solution.py
@@ -294,19 +294,19 @@
     def send_halos():
         x_lo = (me_s, lax.rem(me_c + N_CROSS - 1, N_CROSS))
         x_hi = (me_s, lax.rem(me_c + 1, N_CROSS))
-        for g in range(N_GAS):
-            at = pl.ds(sum(GAS[:g]), GAS[g])
-            rows = pl.ds(0, GAS[g])
-            halo.append(remote(placed[g].at[0, rows], xh.at[at], hsem.at[2 * g], x_lo))
-            halo.append(remote(placed[g].at[BE - 1, rows], xl.at[at], hsem.at[2 * g + 1], x_hi))
+        spans = [(0, 0, 1), (0, 3, GAS[0] - 3)] + [(g, 0, GAS[g]) for g in range(1, N_GAS)]
+        for k, (g, row, count) in enumerate(spans):
+            at, rows = pl.ds(sum(GAS[:g]) + row, count), pl.ds(row, count)
+            halo.append(remote(placed[g].at[0, rows], xh.at[at], hsem.at[2 * k], x_lo))
+            halo.append(remote(placed[g].at[BE - 1, rows], xl.at[at], hsem.at[2 * k + 1], x_hi))
         for copy in halo:
             copy.start()
         pack_z(placed, z0, z15)
         z_lo = (slab(N_SLAB - 1), me_c)
         z_hi = (slab(1), me_c)
         for copy in (
-            remote(z0, zh, hsem.at[2 * N_GAS], z_lo),
-            remote(z15, zl, hsem.at[2 * N_GAS + 1], z_hi),
+            remote(z0, zh, hsem.at[2 * N_GAS + 2], z_lo),
+            remote(z15, zl, hsem.at[2 * N_GAS + 3], z_hi),
         ):
             copy.start()
             halo.append(copy)
@@ -436,7 +436,7 @@
             pltpu.SemaphoreType.DMA((2,)),
             pltpu.SemaphoreType.DMA((len(GROUPS), 2)),
             pltpu.SemaphoreType.DMA((len(GROUPS), 2)),
-            pltpu.SemaphoreType.DMA((2 * N_GAS + 2, 2)),
+            pltpu.SemaphoreType.DMA((2 * N_GAS + 4, 2)),
             pltpu.SemaphoreType.DMA((2, 2)),
             pltpu.SemaphoreType.DMA((len(GROUPS) + 1,)),
             pltpu.VMEM((1, PAR_DEV), F32),

time: 88.8 us -> 88.3 us (level)
  no operation moved by 1% of the time
where the time goes in v6:
time: 88.3 us; the launch traced here: 88.2 us
  Pallas kernels  86.9 us (98%)
  between operations  1.29 us (1%)
    pallas_call x1, Pallas kernels, step(): pl.pallas_call(step_kernel, out_shape=[pltpu.VMEM((FIELDS, BE, 8, 128), F...  85.3 us

profile of v6, /device:TPU:1, one launch (start us, length us, event | category | flops | bytes accessed | tf_op | source)
XLA Modules:
  0.0 88.2 jit_solution(14586869896489889258)
XLA Ops:
  1.3 85.3 %shard_map.113 = (f32[22,16,8,128]{3,2,1,0:T(8,128)S(1)}, f32[22,16,8,128]{3,2,1,0:T(8,128)S(1)}) custom-call(f32[22,16,8,128]{3,2,1,0:T(8,128)} %bitcast.28, f32[3,16,8,128]{3,2,1,0:T(8,128)} %bitcast.30, f32[22,16,8,128]{3,2,1,0:T(8,128)} %bitcast.29, f32[22]{0:T(128)} %d_ref.1, s32[1,4]{1,0:T(1,128)} %tg_ref.1, f32[1,4096]{1,0:T(1,128)} %bitcast.31, ...), custom_call_target="tpu_custom_call" | custom-call | tf_op jit(solution)/shard_map/pallas_call | solution.py:413
  86.6 1.6 %shard_map.114 = (f32[22,16,8,128]{3,2,1,0:T(8,128)}, f32[22,16,8,128]{3,2,1,0:T(8,128)}) custom-call(f32[22,16,8,128]{3,2,1,0:T(8,128)S(1)} %get-tuple-element.6.a_ref, f32[22,16,8,128]{3,2,1,0:T(8,128)S(1)} %get-tuple-element.7.b_ref), custom_call_target="tpu_custom_call" | custom-call | tf_op jit(solution)/shard_map/pallas_call | solution.py:468
